TPU v7x, 512 devices: a whole 4x4x16 slice. The times are simulated.
512 devices in a mesh: seq: 8 (over z_lo), exp: 64 (over x, z_hi, y, core).
Axes of the slice: x: 4, y: 4, z: 16 (z_hi: 2, z_lo: 8; z = z_hi * 8 + z_lo), core: 2. Of those that a mesh axis runs over, the one named last changes fastest.
Arguments:
- queries: bfloat16 [64, 512, 4096], P('exp', 'seq'), may hold values from -160 to 160
- key_heads: bfloat16 [64, 512, 512], P('exp', 'seq'), may hold values from -4 to 4
- value_heads: bfloat16 [64, 512, 512], P('exp', 'seq'), may hold values from -4 to 4
- doc_ids: int32 [64, 512], P('exp'), may hold values from 0 to 7, never falling along the last dimension, each value on 1 to 256 neighbouring positions
- residual: bfloat16 [64, 512, 2048], P('exp', 'seq'), may hold values from -10 to 10
- w_out: bfloat16 [4096, 2048], P('seq'), may hold values from -0.375 to 0.375
- norm_gain: float32 [2048], replicated, may hold values from 0.1 to 1.9
- router_logits: float32 [64, 512, 64], P('exp', 'seq'), may hold values from -12 to 305
- expert_ids: int32 [64, 512, 8], P('exp', 'seq'), may hold values from 0 to 63, as said below
- keep_mask: int32 [64, 512, 8], P('exp', 'seq'), may hold values from 0 to 1, as said below
- w_gate: bfloat16 [64, 768, 2048], P('exp', 'seq'), may hold values from -0.125 to 0.125
- w_up: bfloat16 [64, 768, 2048], P('exp', 'seq'), may hold values from -0.125 to 0.125
- w_down: bfloat16 [64, 768, 2048], P('exp', 'seq'), may hold values from -0.21875 to 0.21875
Outputs:
- hidden: bfloat16 [64, 512, 2048], P('exp', 'seq')
- expert_out: bfloat16 [64, 512, 2048], P('exp', 'seq')
Inputs may be any that keep to these rules, and one draw needn't show every extreme that they name: `expert_ids`: each token names 8 different experts. `keep_mask`: take the assignments of one device's 64 positions of a sequence in order of position and then along the last dimension: an assignment is kept exactly when fewer than 8 earlier ones of that device name the same expert. So at most 8 kept assignments of one device name one expert; other experts may have fewer. In every draw there is an expert, the same one for all devices, that has exactly 8 kept assignments from every device.
All inputs are finite; a program needn't handle non-finite values.
Results may differ from a plain program's by a relative error of at most 0.029.
Values may be sent and summed in bfloat16 or wider, within the bound.
A program may use at most 64 MiB of HBM per device.

v0:
```python
import jax
import jax.numpy as jnp
from jax import lax
from jax.sharding import PartitionSpec as P

HD = 128
TOPK = 8


epsilon = 1e-06


def expert_slice(slot_rows, pieces):
    gate_w, up_w, down_w = pieces
    gate_val = jnp.einsum("esd,ehd->esh", slot_rows, gate_w, preferred_element_type=jnp.float32)
    up_val = jnp.einsum("esd,ehd->esh", slot_rows, up_w, preferred_element_type=jnp.float32)
    act_rows = (jax.nn.silu(gate_val) * up_val).astype(jnp.bfloat16)
    return jnp.einsum("esh,ehd->esd", act_rows, down_w, preferred_element_type=jnp.float32)


def shards(
    queries,
    key_heads,
    value_heads,
    doc_ids,
    residual,
    w_out,
    norm_gain,
    router_logits,
    expert_ids,
    keep_mask,
    w_gate,
    w_up,
    w_down,
):
    seq_size = lax.axis_size("seq")
    tokens = queries.shape[1]
    model_width = residual.shape[2]
    query_rows = queries[0]
    kv_count = key_heads.shape[2] // HD
    copies = max(1, seq_size // kv_count)
    key_rep = jnp.repeat(key_heads[0].reshape(tokens, kv_count, HD), copies, axis=1).reshape(
        tokens, kv_count * copies * HD
    )
    value_rep = jnp.repeat(value_heads[0].reshape(tokens, kv_count, HD), copies, axis=1).reshape(
        tokens, kv_count * copies * HD
    )
    query_seq, key_seq, value_seq = (
        lax.all_to_all(query_rows, "seq", split_axis=1, concat_axis=0, tiled=True),
        lax.all_to_all(key_rep, "seq", split_axis=1, concat_axis=0, tiled=True),
        lax.all_to_all(value_rep, "seq", split_axis=1, concat_axis=0, tiled=True),
    )
    length = query_seq.shape[0]
    local_heads = query_seq.shape[1] // HD
    kv_local = key_seq.shape[1] // HD
    group_size = local_heads // kv_local
    q_grid = query_seq.reshape(length, kv_local, group_size, HD)
    k_grid = key_seq.reshape(length, kv_local, HD)
    v_grid = value_seq.reshape(length, kv_local, HD)
    score_values = jnp.einsum(
        "qhgd,khd->hgqk", q_grid, k_grid, preferred_element_type=jnp.float32
    ) * (1.0 / HD**0.5)
    position = jnp.arange(length, dtype=jnp.int32)
    doc_row = doc_ids[0]
    allowed = (position[None, :] <= position[:, None]) & (doc_row[None, :] == doc_row[:, None])
    score_values = jnp.where(allowed, score_values, -jnp.inf)
    exp_terms = jnp.exp(score_values - jnp.max(score_values, axis=-1, keepdims=True))
    prob_rows = (exp_terms / jnp.sum(exp_terms, axis=-1, keepdims=True)).astype(jnp.bfloat16)
    attended = jnp.einsum("hgqk,khd->qhgd", prob_rows, v_grid, preferred_element_type=jnp.float32)
    attended = attended.reshape(length, local_heads * HD).astype(jnp.bfloat16)
    projected = lax.psum_scatter(
        jnp.dot(attended, w_out, preferred_element_type=jnp.float32).astype(jnp.bfloat16),
        "seq",
        scatter_dimension=0,
        tiled=True,
    ).astype(jnp.float32)
    hidden = residual[0].astype(jnp.float32) + projected
    square = jnp.mean(hidden * hidden, axis=-1, keepdims=True)
    normed = (hidden * lax.rsqrt(square + epsilon) * norm_gain).astype(jnp.bfloat16)
    id_rows = expert_ids[0]
    keep_rows = keep_mask[0]
    logit_rows = router_logits[0]
    experts_all = logit_rows.shape[1]
    capacity = tokens * TOPK // experts_all
    expert_span_indices = jnp.arange(experts_all, dtype=jnp.int32)
    matches = id_rows[:, :, None] == expert_span_indices
    chosen = jnp.sum(jnp.where(matches, logit_rows[:, None, :], 0.0), axis=-1)
    gate_terms = jnp.exp(chosen - jnp.max(chosen, axis=-1, keepdims=True))
    gate_probs = gate_terms / jnp.sum(gate_terms, axis=-1, keepdims=True)
    weights = (gate_probs * keep_rows.astype(jnp.float32)).astype(jnp.bfloat16)
    kept_hits = (
        (matches & (keep_rows[:, :, None] == 1))
        .astype(jnp.int32)
        .reshape(tokens * TOPK, experts_all)
    )
    before = jnp.cumsum(kept_hits, axis=0, dtype=jnp.int32) - kept_hits
    slot_index = jnp.sum(before * kept_hits, axis=-1, dtype=jnp.int32).reshape(tokens, TOPK)
    columns = experts_all * capacity
    placed = (
        (id_rows * capacity + slot_index)[:, :, None] == jnp.arange(columns, dtype=jnp.int32)
    ) & (keep_rows[:, :, None] == 1)
    sender = jnp.any(placed, axis=1).astype(jnp.bfloat16)
    combiner = jnp.sum(jnp.where(placed, weights[:, :, None], jnp.zeros((), jnp.bfloat16)), axis=1)
    outgoing = lax.dot_general(
        sender, normed, (((0,), (0,)), ((), ())), preferred_element_type=jnp.float32
    )
    outgoing = outgoing.astype(jnp.bfloat16).reshape(experts_all, capacity, model_width)
    exp_size = lax.axis_size("exp")
    local_experts = w_gate.shape[0]
    received = lax.all_to_all(outgoing, "exp", split_axis=0, concat_axis=0, tiled=True)
    slot_rows = jnp.swapaxes(received.reshape(exp_size, local_experts, capacity, model_width), 0, 1)
    slot_rows = slot_rows.reshape(local_experts, exp_size * capacity, model_width)
    produced = expert_slice(
        slot_rows,
        (
            lax.all_gather(w_gate, "seq", axis=1, tiled=True),
            lax.all_gather(w_up, "seq", axis=1, tiled=True),
            lax.all_gather(w_down, "seq", axis=1, tiled=True),
        ),
    )
    returned = jnp.swapaxes(
        produced.astype(jnp.bfloat16).reshape(local_experts, exp_size, capacity, model_width), 0, 1
    )
    returned = returned.reshape(exp_size * local_experts, capacity, model_width)
    returned_rows = lax.all_to_all(returned, "exp", split_axis=0, concat_axis=0, tiled=True)
    expert_out = jnp.dot(
        combiner, returned_rows.reshape(columns, model_width), preferred_element_type=jnp.float32
    ).astype(jnp.bfloat16)
    return (hidden.astype(jnp.bfloat16)[None], expert_out[None])


def solution(mesh):
    placed = (
        P("exp", "seq", None),
        P("exp", "seq", None),
        P("exp", "seq", None),
        P("exp", None),
        P("exp", "seq", None),
        P("seq", None),
        P(),
        P("exp", "seq", None),
        P("exp", "seq", None),
        P("exp", "seq", None),
        P("exp", "seq", None),
        P("exp", "seq", None),
        P("exp", "seq", None),
    )
    return jax.shard_map(
        shards,
        mesh=mesh,
        in_specs=placed,
        out_specs=(P("exp", "seq", None), P("exp", "seq", None)),
        check_vma=False,
    )
```

profile of v0, /device:TPU:97, one launch (start us, length us, event | category | flops | bytes accessed | tf_op | source)
XLA Modules:
  0.0 624.0 jit_solution(7096127187506463661)
XLA Ops:
  7.2 1.4 copy.54
  9.5 11.2 %all-to-all-start.1 = ((bf16[64,8,512]{2,0,1:T(8,128)(2,1)}), bf16[64,8,512]{2,0,1:T(8,128)(2,1)S(1)}, u32[]{:S(2)}, u32[]{:S(2)}) async-start(bf16[64,8,512]{2,0,1:T(8,128)(2,1)} %copy.37), calls=%async_computation.1 | async-start | bytes 1048576 | tf_op jit(solution)/shard_map/all_to_all | solution.py:49
  20.7 22.1 %all-to-all-done.1 = bf16[64,8,512]{2,0,1:T(8,128)(2,1)S(1)} async-done(((bf16[64,8,512]{2,0,1:T(8,128)(2,1)}), bf16[64,8,512]{2,0,1:T(8,128)(2,1)S(1)}, u32[]{:S(2)}, u32[]{:S(2)}) %all-to-all-start.1) | async-done | bytes 524320 | tf_op jit(solution)/shard_map/all_to_all | solution.py:49
  43.5 10.4 %all-to-all-start = ((bf16[64,8,128]{2,0,1:T(8,128)(2,1)}), bf16[64,8,128]{2,0,1:T(8,128)(2,1)S(1)}, u32[]{:S(2)}, u32[]{:S(2)}) async-start(bf16[64,8,128]{2,0,1:T(8,128)(2,1)} %bitcast.2), calls=%async_computation | async-start | bytes 262144 | tf_op jit(solution)/shard_map/all_to_all | solution.py:50
  55.0 6.5 %all-to-all-done = bf16[64,8,128]{2,0,1:T(8,128)(2,1)S(1)} async-done(((bf16[64,8,128]{2,0,1:T(8,128)(2,1)}), bf16[64,8,128]{2,0,1:T(8,128)(2,1)S(1)}, u32[]{:S(2)}, u32[]{:S(2)}) %all-to-all-start) | async-done | bytes 131104 | tf_op jit(solution)/shard_map/all_to_all | solution.py:50
  61.5 1.5 broadcast_in_dim.61
  63.0 8.0 %all-to-all-start.2 = ((bf16[64,8,128]{2,0,1:T(8,128)(2,1)}), bf16[64,8,128]{2,0,1:T(8,128)(2,1)S(1)}, u32[]{:S(2)}, u32[]{:S(2)}) async-start(bf16[64,8,128]{2,0,1:T(8,128)(2,1)} %bitcast.10), calls=%async_computation.2 | async-start | bytes 262144 | tf_op jit(solution)/shard_map/all_to_all | solution.py:51
  71.9 1.9 copy-done.1
  74.7 3.8 all-to-all-done.2
  78.5 3.4 fusion.26
  82.0 2.6 convolution_convert_fusion.1
  86.7 1.2 reduce-window.6
  89.0 53.8 %reduce-scatter.2.cloned.1.call-done = bf16[64,2048]{1,0:T(8,128)(2,1)} async-done(((bf16[512,2048]{1,0:T(8,128)(2,1)}), bf16[64,2048]{1,0:T(8,128)(2,1)}) %reduce-scatter.2.cloned.1.call-update) | async-done | bytes 262160 | tf_op jit(solution)/shard_map/reduce_scatter | solution.py:71
  142.9 1.8 multiply_reduce_fusion
  144.7 3.2 fusion.11
  147.9 19.5 %all-to-all-start.3 = ((bf16[64,8,2048]{2,1,0:T(8,128)(2,1)}), bf16[64,8,2048]{2,1,0:T(8,128)(2,1)}, u32[]{:S(2)}, u32[]{:S(2)}) async-start(bf16[64,8,2048]{2,1,0:T(8,128)(2,1)} %fusion.11), calls=%async_computation.4 | async-start | bytes 4194304 | tf_op jit(solution)/shard_map/all_to_all | solution.py:110
  168.0 150.6 %all-gather.4.cloned.1.call-done = bf16[1,768,2048]{2,1,0:T(8,128)(2,1)} async-done(((bf16[1,96,2048]{2,1,0:T(8,128)(2,1)}), bf16[1,768,2048]{2,1,0:T(8,128)(2,1)}) %all-gather.4.cloned.1.call-update) | async-done | bytes 3145744 | tf_op jit(solution)/shard_map/all_gather | solution.py:116
  318.6 5.5 fusion.6
  324.2 77.8 %all-gather.8.cloned.1.call-done = bf16[1,768,2048]{2,1,0:T(8,128)(2,1)} async-done(((bf16[1,96,2048]{2,1,0:T(8,128)(2,1)}), bf16[1,768,2048]{2,1,0:T(8,128)(2,1)}) %all-gather.8.cloned.1.call-update) | async-done | bytes 3145744 | tf_op jit(solution)/shard_map/all_gather | solution.py:118
  401.9 80.9 %all-gather.6.cloned.1.call-done = bf16[1,768,2048]{2,1,0:T(8,128)(2,1)} async-done(((bf16[1,96,2048]{2,1,0:T(8,128)(2,1)}), bf16[1,768,2048]{2,1,0:T(8,128)(2,1)}) %all-gather.6.cloned.1.call-update) | async-done | bytes 3145744 | tf_op jit(solution)/shard_map/all_gather | solution.py:117
  482.9 9.3 %fusion.12 = bf16[64,8,2048]{2,1,0:T(8,128)(2,1)} fusion(bf16[1,768,2048]{2,1,0:T(8,128)(2,1)} %all-gather.8.cloned.1.call-done, f32[512,768]{1,0:T(8,128)} %fusion.6, bf16[1,768,2048]{2,1,0:T(8,128)(2,1)} %all-gather.6.cloned.1.call-done, bf16[64,8,2048]{2,1,0:T(8,128)(2,1)} %all-to-all-done.3), kind=kOutput, calls=%fused_computation.15 | convolution fusion | flops 3224633344 | bytes 12058624 | tf_op jit(solution)/shard_map/esh,ehd->esd/dot_general | solution.py:18
  492.1 16.0 %all-to-all-start.4 = ((bf16[64,8,2048]{2,1,0:T(8,128)(2,1)}), bf16[64,8,2048]{2,1,0:T(8,128)(2,1)}, u32[]{:S(2)}, u32[]{:S(2)}) async-start(bf16[64,8,2048]{2,1,0:T(8,128)(2,1)} %fusion.12), calls=%async_computation.5 | async-start | bytes 4194304 | tf_op jit(solution)/shard_map/all_to_all | solution.py:125
  509.4 105.3 %all-to-all-done.4 = bf16[64,8,2048]{2,1,0:T(8,128)(2,1)} async-done(((bf16[64,8,2048]{2,1,0:T(8,128)(2,1)}), bf16[64,8,2048]{2,1,0:T(8,128)(2,1)}, u32[]{:S(2)}, u32[]{:S(2)}) %all-to-all-start.4) | async-done | bytes 2097184 | tf_op jit(solution)/shard_map/all_to_all | solution.py:125
  614.7 2.8 fusion.15
  (62 shorter events, 9.4 us)
Async XLA Ops:
  7.2 74.8 %copy-start = (bf16[512,2048]{1,0:T(8,128)(2,1)S(1)}, bf16[512,2048]{1,0:T(8,128)(2,1)}, u32[]{:S(2)}) copy-start(bf16[512,2048]{1,0:T(8,128)(2,1)} %param.18) | copy-start | bytes 6291460
  7.2 13.5 %copy-start.3 = (bf16[1,64,512]{2,1,0:T(8,128)(2,1)S(1)}, bf16[1,64,512]{2,1,0:T(8,128)(2,1)}, u32[]{:S(2)}) copy-start(bf16[1,64,512]{2,1,0:T(8,128)(2,1)} %param.14) | copy-start | bytes 196612
  7.2 46.8 %copy-start.4 = (bf16[1,64,512]{2,1,0:T(8,128)(2,1)S(1)}, bf16[1,64,512]{2,1,0:T(8,128)(2,1)}, u32[]{:S(2)}) copy-start(bf16[1,64,512]{2,1,0:T(8,128)(2,1)} %param.15) | copy-start | bytes 196612
  7.2 47.4 %copy-start.8 = (s32[1,512]{1,0:T(1,128)S(1)}, s32[1,512]{1,0:T(1,128)}, u32[]{:S(2)}) copy-start(s32[1,512]{1,0:T(1,128)} %param.16) | copy-start | bytes 6148
  9.5 33.4 %all-to-all-start.1 = ((bf16[64,8,512]{2,0,1:T(8,128)(2,1)}), bf16[64,8,512]{2,0,1:T(8,128)(2,1)S(1)}, u32[]{:S(2)}, u32[]{:S(2)}) async-start(bf16[64,8,512]{2,0,1:T(8,128)(2,1)} %copy.37), calls=%async_computation.1 | async-start | bytes 1048576 | tf_op jit(solution)/shard_map/all_to_all | solution.py:49
  43.5 17.9 %all-to-all-start = ((bf16[64,8,128]{2,0,1:T(8,128)(2,1)}), bf16[64,8,128]{2,0,1:T(8,128)(2,1)S(1)}, u32[]{:S(2)}, u32[]{:S(2)}) async-start(bf16[64,8,128]{2,0,1:T(8,128)(2,1)} %bitcast.2), calls=%async_computation | async-start | bytes 262144 | tf_op jit(solution)/shard_map/all_to_all | solution.py:50
  63.0 15.5 %all-to-all-start.2 = ((bf16[64,8,128]{2,0,1:T(8,128)(2,1)}), bf16[64,8,128]{2,0,1:T(8,128)(2,1)S(1)}, u32[]{:S(2)}, u32[]{:S(2)}) async-start(bf16[64,8,128]{2,0,1:T(8,128)(2,1)} %bitcast.10), calls=%async_computation.2 | async-start | bytes 262144 | tf_op jit(solution)/shard_map/all_to_all | solution.py:51
  71.0 71.8 %reduce-scatter.2.cloned.1.call-start = ((), (), s32[]{:S(2)}) async-start(), calls=%async_computation.6 | async-start | bytes 2359296 | tf_op jit(solution)/shard_map/reduce_scatter | solution.py:71
  71.9 1.9 copy-start.1
  81.9 4.2 copy-start.9
  82.0 4.4 copy-start.5
  84.6 58.3 %copy-start.2 = (bf16[1,64,2048]{2,1,0:T(8,128)(2,1)S(1)}, bf16[1,64,2048]{2,1,0:T(8,128)(2,1)}, u32[]{:S(2)}) copy-start(bf16[1,64,2048]{2,1,0:T(8,128)(2,1)} %param.17) | copy-start | bytes 786436
  84.6 60.1 %copy-start.7 = (f32[2048]{0:T(1024)S(1)}, f32[2048]{0:T(1024)}, u32[]{:S(2)}) copy-start(f32[2048]{0:T(1024)} %param.19) | copy-start | bytes 24580
  84.6 234.0 %all-gather.4.cloned.1.call-start = ((), (), s32[]{:S(2)}) async-start(), calls=%async_computation.7 | async-start | bytes 3538944 | tf_op jit(solution)/shard_map/all_gather | solution.py:116
  85.4 316.6 %all-gather.8.cloned.1.call-start = ((), (), s32[]{:S(2)}) async-start(), calls=%async_computation.9 | async-start | bytes 3538944 | tf_op jit(solution)/shard_map/all_gather | solution.py:118
  147.9 170.7 %all-to-all-start.3 = ((bf16[64,8,2048]{2,1,0:T(8,128)(2,1)}), bf16[64,8,2048]{2,1,0:T(8,128)(2,1)}, u32[]{:S(2)}, u32[]{:S(2)}) async-start(bf16[64,8,2048]{2,1,0:T(8,128)(2,1)} %fusion.11), calls=%async_computation.4 | async-start | bytes 4194304 | tf_op jit(solution)/shard_map/all_to_all | solution.py:110
  167.4 315.4 %all-gather.6.cloned.1.call-start = ((), (), s32[]{:S(2)}) async-start(), calls=%async_computation.8 | async-start | bytes 3538944 | tf_op jit(solution)/shard_map/all_gather | solution.py:117
  492.1 16.1 %copy-start.6 = (f32[1,64,64]{2,1,0:T(8,128)S(1)}, f32[1,64,64]{2,1,0:T(8,128)}, u32[]{:S(2)}) copy-start(f32[1,64,64]{2,1,0:T(8,128)} %param.20) | copy-start | bytes 49156
  492.1 122.6 %all-to-all-start.4 = ((bf16[64,8,2048]{2,1,0:T(8,128)(2,1)}), bf16[64,8,2048]{2,1,0:T(8,128)(2,1)}, u32[]{:S(2)}, u32[]{:S(2)}) async-start(bf16[64,8,2048]{2,1,0:T(8,128)(2,1)} %fusion.12), calls=%async_computation.5 | async-start | bytes 4194304 | tf_op jit(solution)/shard_map/all_to_all | solution.py:125
Sparse Core Ops, SparseCore 0:
  84.7 58.0 reduce-scatter.1
  144.9 173.6 all-gather.3
  320.7 81.1 all-gather.7
  403.9 78.9 all-gather.5
where the time goes:
time: 625 us; the launch traced here: 624 us
  waiting for transfers between devices  503 us (80%)
  starting transfers between devices  65.5 us (10%)
  matrix products  27.7 us (4%)
  between operations  14 us (2%)
  local copies, waits for them, and re-layouts  8.36 us (1%)
    all_gather x1, waiting for transfers between devices, shards(): lax.all_gather(w_gate, 'seq', axis=1, tiled=True)  151 us
    all_to_all x1, waiting for transfers between devices, shards(): lax.all_to_all(returned, 'exp', split_axis=0, concat_axis=0, tiled=True)  105 us
    all_gather x1, waiting for transfers between devices, shards(): lax.all_gather(w_up, 'seq', axis=1, tiled=True)  80.9 us
    all_gather x1, waiting for transfers between devices, shards(): lax.all_gather(w_down, 'seq', axis=1, tiled=True)  77.8 us
    reduce_scatter x1, waiting for transfers between devices, shards(): lax.psum_scatter(jnp.dot(attended, w_out, preferred_element_type=jnp.floa...  53.8 us
    all_to_all x1, waiting for transfers between devices, shards(): lax.all_to_all(query_rows, 'seq', split_axis=1, concat_axis=0, tiled=True)  22.1 us
    all_to_all x1, starting transfers between devices, shards(): lax.all_to_all(outgoing, 'exp', split_axis=0, concat_axis=0, tiled=True)  19.5 us
    all_to_all x1, starting transfers between devices, shards(): lax.all_to_all(returned, 'exp', split_axis=0, concat_axis=0, tiled=True)  16 us
  transfers between devices with their start and end apart: 9, of which 8 were waited for; matrix products, arithmetic and copies ran while one was open for 3% of the time, Pallas kernels for 0%

commit v1 on v0

v1 whole, which is shorter than its diff:
```python
import functools

import jax
import jax.numpy as jnp
from jax import lax
from jax.experimental import pallas as pl
from jax.experimental.pallas import tpu as pltpu
from jax.sharding import PartitionSpec as P

MESH = pl.DeviceIdType.MESH
HD = 128
CAP = 8
X, Y, Z, LINE, CORES = 4, 4, 16, 8, 2
PLANE = X * Y * CORES
SUB = 4
CHUNKS = 4
EPSILON = 1e-06
NEG = -1e30
ANY = pl.BlockSpec(memory_space=pl.ANY)
VMEM = pl.BlockSpec(memory_space=pltpu.VMEM)


def place():
    s = lax.axis_index("seq")
    e = lax.axis_index("exp")
    c = e % 2
    y = (e // 2) % Y
    zh = (e // (2 * Y)) % 2
    x = e // (4 * Y)
    return x, y, zh * LINE + s, c


def device(x, y, z, c):
    x, y, z = x % X, y % Y, z % Z
    return {"seq": z % LINE, "exp": ((x * 2 + z // LINE) * Y + y) * 2 + c}


def rows(start, count):
    return pl.ds(pl.multiple_of(start, 16), count)


def meet(peers):
    barrier = pltpu.get_barrier_semaphore()
    for peer in peers:
        pl.semaphore_signal(barrier, inc=1, device_id=peer, device_id_type=MESH)
    pl.semaphore_wait(barrier, len(peers))


Z_OFFSETS = (1, -1, 2, -2, 3, -3, 4)


def front_kernel(
    q_ref, k_ref, v_ref, bias_ref, res_ref, gain_ref, meta_ref, wout_ref, wg_ref, wu_ref, wd_ref,
    hidden_ref, normed_ref, wts_ref, metas_ref,
    wbuf, kv, att, total, send, recv, local,
):
    x, y, z, c = place()
    s = z % LINE
    p = z % SUB
    at = lambda dx=0, dy=0, dz=0: device(x + dx + X, y + dy + Y, z + dz + Z, c)
    sibling = device(x, y, z, 1 - c)
    counter = [0]

    def remote(src, dst, peer):
        i = counter[0]
        counter[0] += 1
        return pltpu.make_async_remote_copy(
            src_ref=src, dst_ref=dst, send_sem=send.at[i], recv_sem=recv.at[i],
            device_id=peer, device_id_type=MESH,
        )

    meet(
        [at(dz=d) for d in (1, -1, 2, -2, 3, -3, 4, -4, 8)]
        + [at(dx=1), at(dx=-1), at(dy=1), at(dy=-1), sibling]
    )

    pending = []
    kv[4, 0] = k_ref[...]
    kv[4, 1] = v_ref[...]
    kv_steps = [remote(kv.at[4 - d], kv.at[3 - d], at(dz=1)) for d in range(4)]
    kv_steps[0].start()

    ja = (y * 2 + c) * X + x
    jb = (x * 2 + c) * Y + y
    mine = jnp.where(s < 4, ja, jb) * 16
    piece = wbuf.at[s, rows(mine, 16)]
    own = pltpu.make_async_copy(wout_ref.at[rows(mine, 16)], piece, local.at[0])
    own.start()
    z_copies = [remote(wout_ref.at[rows(mine, 16)], piece, at(dz=d)) for d in Z_OFFSETS]
    for copy in z_copies:
        copy.start()
    zh = z // LINE
    metas_ref[0] = meta_ref[zh]
    meta_copies = [
        remote(meta_ref.at[1 - zh], metas_ref.at[3], at(dz=8)),
        remote(meta_ref.at[((z + 4) % Z) // LINE], metas_ref.at[1], at(dz=4)),
        remote(meta_ref.at[((z + 12) % Z) // LINE], metas_ref.at[2], at(dz=-4)),
    ]
    for copy in meta_copies:
        copy.start()
    for m, ref in enumerate((wg_ref, wu_ref, wd_ref)):
        pltpu.make_async_copy(ref, wts_ref.at[m, rows(96 * p, 96)], local.at[1 + m]).start()
    for m, ref in enumerate((wg_ref, wu_ref, wd_ref)):
        pltpu.make_async_copy(ref, wts_ref.at[m, rows(96 * p, 96)], local.at[1 + m]).wait()
    kv_steps[0].wait_recv()
    kv_steps[1].start()
    own.wait()
    for copy in z_copies:
        copy.wait_recv()

    def block(owner):
        return wts_ref.at[:, rows(96 * ((owner + SUB) % SUB), 96)]

    up1 = remote(block(p), block(p), at(dz=1))
    down1 = remote(block(p), block(p), at(dz=-1))
    up2 = remote(block(p - 1), block(p - 1), at(dz=1))
    down2 = remote(block(p + 1), block(p + 1), at(dz=-1))

    def ring(region, lo, step):
        first = [remote(region(0, lo, 4), region(0, lo, 4), step(d)) for d in (1, -1)]
        second = [
            remote(region(-1, lo, 2), region(-1, lo, 2), step(1)),
            remote(region(1, lo + 2, 2), region(1, lo + 2, 2), step(-1)),
        ]
        return first, second

    def region_ax(d, lo, n):
        return wbuf.at[pl.ds(lo, n), rows(16 * ((y * 2 + c) * X + (x + d + X) % X), 16)]

    def region_by(d, lo, n):
        return wbuf.at[pl.ds(lo, n), rows(16 * ((x * 2 + c) * Y + (y + d + Y) % Y), 16)]

    def region_ay(d, lo, n):
        return wbuf.at[pl.ds(lo, n), rows(64 * (((y + d + Y) % Y) * 2 + c), 64)]

    def region_bx(d, lo, n):
        return wbuf.at[pl.ds(lo, n), rows(64 * (((x + d + X) % X) * 2 + c), 64)]

    step_x = lambda d: at(dx=d)
    step_y = lambda d: at(dy=d)
    a1, a2 = ring(region_ax, 0, step_x)
    b1, b2 = ring(region_by, 4, step_y)
    for copy in a1 + b1:
        copy.start()
    pl.when(p < 3)(up1.start)
    pl.when(p > 0)(down1.start)
    kv_steps[1].wait_recv()
    kv_steps[2].start()
    for copy in a1 + b1:
        copy.wait_recv()
    for copy in a2 + b2:
        copy.start()
    kv_steps[2].wait_recv()
    kv_steps[3].start()
    for copy in a2 + b2:
        copy.wait_recv()
    c1, c2 = ring(region_ay, 0, step_y)
    d1, d2 = ring(region_bx, 4, step_x)
    twins = {
        d: [
            remote(region_ay(d, 0, 4), region_ay(d, 0, 4), sibling),
            remote(region_bx(d, 4, 4), region_bx(d, 4, 4), sibling),
        ]
        for d in (0, 1, -1, 2)
    }
    for copy in c1 + d1 + twins[0]:
        copy.start()
    kv_steps[3].wait_recv()

    groups = 4
    for g in range(groups):
        head = lambda h: (g * 8 + h) * HD
        queries = jnp.concatenate([q_ref[:, head(h):head(h) + HD] for h in range(8)], axis=0)
        keys = kv[:, 0, :, g * HD:(g + 1) * HD].reshape(5 * 64, HD)
        values = kv[:, 1, :, g * HD:(g + 1) * HD].reshape(5 * 64, HD)
        scores = lax.dot_general(
            queries, keys, (((1,), (1,)), ((), ())), preferred_element_type=jnp.float32
        ) * (1.0 / HD**0.5)
        scores = scores.reshape(8, 64, 320) + bias_ref[...][None]
        scores = scores.reshape(512, 320)
        terms = jnp.exp(scores - jnp.max(scores, axis=-1, keepdims=True))
        probs = (terms / jnp.sum(terms, axis=-1, keepdims=True)).astype(jnp.bfloat16)
        out = jnp.dot(probs, values, preferred_element_type=jnp.float32).astype(jnp.bfloat16)
        for h in range(8):
            att[:, head(h):head(h) + HD] = out[64 * h:64 * (h + 1)]

    for copy in c1 + d1:
        copy.wait_recv()
    for copy in c2 + d2 + twins[1] + twins[-1]:
        copy.start()
    pl.when(p > 0)(up1.wait_recv)
    pl.when(p < 3)(down1.wait_recv)
    pl.when((p > 0) & (p < 3))(up2.start)
    pl.when((p > 0) & (p < 3))(down2.start)
    for copy in c2 + d2:
        copy.wait_recv()
    for copy in twins[2]:
        copy.start()
    for d in (0, 1, -1, 2):
        for copy in twins[d]:
            copy.wait_recv()

    for n in range(4):
        cols = slice(512 * n, 512 * (n + 1))
        acc = res_ref[:, cols].astype(jnp.float32)
        for t in range(8):
            acc = acc + jnp.dot(
                att[:, 512 * t:512 * (t + 1)], wbuf[t, :, cols], preferred_element_type=jnp.float32
            )
        total[:, cols] = acc
    hidden = total[...]
    hidden_ref[...] = hidden.astype(jnp.bfloat16)
    square = jnp.mean(hidden * hidden, axis=-1, keepdims=True)
    normed_ref[...] = (hidden * lax.rsqrt(square + EPSILON) * gain_ref[...]).astype(jnp.bfloat16)

    for copy in meta_copies:
        copy.wait_recv()
    pl.when(p > 1)(up2.wait_recv)
    pl.when(p < 2)(down2.wait_recv)
    for copy in kv_steps + z_copies + meta_copies + a1 + b1 + a2 + b2 + c1 + d1 + c2 + d2:
        copy.wait_send()
    for d in (0, 1, -1, 2):
        for copy in twins[d]:
            copy.wait_send()
    pl.when(p < 3)(up1.wait_send)
    pl.when(p > 0)(down1.wait_send)
    pl.when((p > 0) & (p < 3))(up2.wait_send)
    pl.when((p > 0) & (p < 3))(down2.wait_send)


def front(q, k, v, bias, res, gain, meta, wout, wg, wu, wd):
    d = res.shape[1]
    copies = 48
    return pl.pallas_call(
        front_kernel,
        out_shape=(
            jax.ShapeDtypeStruct((64, d), jnp.bfloat16),
            jax.ShapeDtypeStruct((64, d), jnp.bfloat16),
            jax.ShapeDtypeStruct((3, SUB * 96, d), jnp.bfloat16),
            jax.ShapeDtypeStruct((4, 64, 128), jnp.float32),
        ),
        in_specs=[VMEM] * 7 + [ANY] * 4,
        out_specs=(VMEM, VMEM, ANY, VMEM),
        scratch_shapes=[
            pltpu.VMEM((LINE, 512, d), jnp.bfloat16),
            pltpu.VMEM((5, 2, 64, 512), jnp.bfloat16),
            pltpu.VMEM((64, 4096), jnp.bfloat16),
            pltpu.VMEM((64, d), jnp.float32),
            pltpu.SemaphoreType.DMA((copies,)),
            pltpu.SemaphoreType.DMA((copies,)),
            pltpu.SemaphoreType.DMA((4,)),
        ],
        compiler_params=pltpu.CompilerParams(
            collective_id=0, has_side_effects=True, vmem_limit_bytes=48 * 2**20
        ),
        cost_estimate=pl.CostEstimate(flops=10**9, bytes_accessed=2 * 10**7, transcendentals=10**6),
    )(q, k, v, bias, res, gain, meta, wout, wg, wu, wd)


def back_kernel(
    normed_ref, metas_ref, wts_ref, out_ref,
    wv, pick, comb, tok, sent, got, accum, act, made, back, part, far, home,
    z_send, z_recv, h_send, h_recv, p_send, p_recv, r_send, r_recv, f_send, f_recv, o_send, o_recv,
    w_send, w_recv, local, selfs,
):
    x, y, z, c = place()
    p = z % SUB
    me = (x * Y + y) * CORES + c
    at = lambda dz: device(x, y, z + dz + Z, c)
    width = tok.shape[2]

    def plane(i):
        return device(i // (Y * CORES), (i // CORES) % Y, z, i % CORES)

    def remote(src, dst, ss, rs, peer):
        return pltpu.make_async_remote_copy(
            src_ref=src, dst_ref=dst, send_sem=ss, recv_sem=rs, device_id=peer, device_id_type=MESH
        )

    barrier = pltpu.get_barrier_semaphore()
    for d in (4, -4, 1, -1):
        pl.semaphore_signal(barrier, inc=1, device_id=at(d), device_id_type=MESH)

    def greet(o, _):
        pl.semaphore_signal(barrier, inc=1, device_id=plane((me + o) % PLANE), device_id_type=MESH)
        return 0

    lax.fori_loop(1, PLANE, greet, 0)
    pl.semaphore_wait(barrier, 4 + PLANE - 1)

    for q in range(CHUNKS):
        tok[q, 0:64] = normed_ref[:, width * q:width * (q + 1)]
    near = [
        (
            remote(tok.at[q, pl.ds(0, 64)], tok.at[q, pl.ds(64, 64)], z_send.at[q, 0], z_recv.at[q, 0], at(4)),
            remote(tok.at[q, pl.ds(0, 64)], tok.at[q, pl.ds(128, 64)], z_send.at[q, 1], z_recv.at[q, 1], at(-4)),
        )
        for q in range(CHUNKS)
    ]
    across = [
        (
            remote(tok.at[q, pl.ds(64, 32)], tok.at[q, pl.ds(192, 32)], h_send.at[q, 0], h_recv.at[q, 0], at(4)),
            remote(tok.at[q, pl.ds(160, 32)], tok.at[q, pl.ds(224, 32)], h_send.at[q, 1], h_recv.at[q, 1], at(-4)),
        )
        for q in range(CHUNKS)
    ]
    for q in range(CHUNKS):
        for copy in near[q]:
            copy.start()

    def block(ref, owner):
        return ref.at[:, pl.ds(96 * owner, 96)]

    up3 = remote(block(wts_ref, 0), block(wv, 0), w_send.at[0], w_recv.at[0], at(1))
    down3 = remote(block(wts_ref, 3), block(wv, 3), w_send.at[1], w_recv.at[1], at(-1))
    pl.when(p == 2)(up3.start)
    pl.when(p == 1)(down3.start)
    keep = [p != 3, None, None, p != 0]
    blocks = [
        pltpu.make_async_copy(block(wts_ref, m), block(wv, m), local.at[m]) for m in range(SUB)
    ]
    for m in range(SUB):
        if keep[m] is None:
            blocks[m].start()
        else:
            pl.when(keep[m])(blocks[m].start)

    for a in range(2):
        lane = lax.broadcasted_iota(jnp.int32, (PLANE, 128), 1)
        slots = jnp.where(lane < 64, metas_ref[2 * a, 0:32], metas_ref[2 * a + 1, 0:32])
        weights = jnp.where(lane < 64, metas_ref[2 * a, 32:64], metas_ref[2 * a + 1, 32:64])
        row = lax.broadcasted_iota(jnp.int32, (PLANE, 4 * CAP, 128), 1)
        column = lax.broadcasted_iota(jnp.int32, (PLANE, 4 * CAP, 128), 2)
        same = row // CAP == 2 * a + column // 64
        hit = same & (slots[:, None, :] == (row % CAP).astype(jnp.float32))
        pick[:, 128 * a:128 * (a + 1)] = (
            jnp.where(hit, 1.0, 0.0).reshape(PLANE * 4 * CAP, 128).astype(jnp.bfloat16)
        )
        comb[:, 128 * a:128 * (a + 1)] = (
            jnp.where(hit, weights[:, None, :], 0.0).reshape(PLANE * 4 * CAP, 128).astype(jnp.bfloat16)
        )

    def spread(src, dst, q, ss, rs):
        def go(o, _):
            peer = (me + o) % PLANE
            remote(
                src.at[q, rows(32 * peer, 32)], dst.at[q, rows(32 * me, 32)], ss.at[q], rs.at[q], plane(peer)
            ).start()
            return 0

        lax.fori_loop(1, PLANE, go, 0)
        dst[q, rows(32 * me, 32)] = src[q, rows(32 * me, 32)]

    def whole(src, dst, q, ss, rs):
        span = pl.ds(0, 32 * (PLANE - 1))
        return remote(src.at[q, span], dst.at[q, span], ss.at[q], rs.at[q], at(1))

    def dispatch(q):
        for copy in across[q]:
            copy.wait_recv()

        def tile(i, _):
            part_rows = pl.ds(pl.multiple_of(i * 256, 256), 256)
            sent[q, part_rows] = jnp.dot(
                pick[part_rows], tok[q], preferred_element_type=jnp.float32
            ).astype(jnp.bfloat16)
            return 0

        lax.fori_loop(0, 4, tile, 0)
        spread(sent, got, q, p_send, p_recv)

    for q in range(CHUNKS):
        for copy in near[q]:
            copy.wait_recv()
        for copy in across[q]:
            copy.start()
        if q >= 1:
            dispatch(q - 1)
    dispatch(CHUNKS - 1)

    for m in range(SUB):
        if keep[m] is None:
            blocks[m].wait()
        else:
            pl.when(keep[m])(blocks[m].wait)
    pl.when(p == 3)(up3.wait_recv)
    pl.when(p == 0)(down3.wait_recv)
    hidden_units = SUB * 96
    transposed = (((1,), (1,)), ((), ()))
    for q in range(CHUNKS):
        whole(sent, got, q, p_send, p_recv).wait_recv()
        cols = slice(width * q, width * (q + 1))

        def tile(i, _, q=q, cols=cols):
            part_rows = pl.ds(pl.multiple_of(i * 256, 256), 256)
            for m in range(2):
                value = lax.dot_general(
                    got[q, part_rows], wv[m, :, cols], transposed, preferred_element_type=jnp.float32
                )
                if q == 0:
                    accum[m, part_rows] = value
                else:
                    accum[m, part_rows] += value
            return 0

        lax.fori_loop(0, 4, tile, 0)

    def activate(i, _):
        part_rows = pl.ds(pl.multiple_of(i * 256, 256), 256)
        gate = accum[0, part_rows]
        act[part_rows] = (gate / (1.0 + jnp.exp(-gate)) * accum[1, part_rows]).astype(jnp.bfloat16)
        return 0

    lax.fori_loop(0, 4, activate, 0)

    for q in range(CHUNKS):
        cols = slice(width * q, width * (q + 1))

        def tile(i, _, q=q, cols=cols):
            part_rows = pl.ds(pl.multiple_of(i * 256, 256), 256)
            made[q, part_rows] = jnp.dot(
                act[part_rows], wv[2, :, cols], preferred_element_type=jnp.float32
            ).astype(jnp.bfloat16)
            return 0

        lax.fori_loop(0, 4, tile, 0)
        spread(made, back, q, r_send, r_recv)

    def half_copies(q):
        return (
            remote(far.at[q, 0, pl.ds(0, 32)], home.at[q, 0, pl.ds(0, 32)], f_send.at[q, 0], f_recv.at[q, 0], at(4)),
            remote(far.at[q, 0, pl.ds(32, 32)], home.at[q, 0, pl.ds(32, 32)], f_send.at[q, 1], f_recv.at[q, 1], at(-4)),
        )

    def home_copies(q):
        return (
            remote(far.at[q, 1], home.at[q, 1], o_send.at[q, 0], o_recv.at[q, 0], at(-4)),
            remote(far.at[q, 2], home.at[q, 2], o_send.at[q, 1], o_recv.at[q, 1], at(4)),
        )

    def combine(q):
        whole(made, back, q, r_send, r_recv).wait_recv()
        part[q] = lax.dot_general(
            comb[...], back[q], (((0,), (0,)), ((), ())), preferred_element_type=jnp.float32
        )
        far[q, 0] = part[q, 192:256].astype(jnp.bfloat16)
        for copy in half_copies(q):
            copy.start()

    def relay(q):
        for copy in half_copies(q):
            copy.wait_recv()
        ahead, behind = part[q, 128:192], part[q, 64:128]
        far[q, 2, 0:32] = (ahead[0:32] + home[q, 0, 0:32].astype(jnp.float32)).astype(jnp.bfloat16)
        far[q, 2, 32:64] = ahead[32:64].astype(jnp.bfloat16)
        far[q, 1, 0:32] = behind[0:32].astype(jnp.bfloat16)
        far[q, 1, 32:64] = (behind[32:64] + home[q, 0, 32:64].astype(jnp.float32)).astype(jnp.bfloat16)
        for copy in home_copies(q):
            copy.start()

    def finish(q):
        for copy in home_copies(q):
            copy.wait_recv()
        total = part[q, 0:64] + home[q, 1].astype(jnp.float32) + home[q, 2].astype(jnp.float32)
        out_ref[:, width * q:width * (q + 1)] = total.astype(jnp.bfloat16)

    for step in range(CHUNKS + 2):
        if step < CHUNKS:
            combine(step)
        if 0 <= step - 1 < CHUNKS:
            relay(step - 1)
        if 0 <= step - 2 < CHUNKS:
            finish(step - 2)

    for q in range(CHUNKS):
        for copy in near[q] + across[q] + half_copies(q) + home_copies(q):
            copy.wait_send()
        whole(sent, got, q, p_send, p_recv).wait_send()
        whole(made, back, q, r_send, r_recv).wait_send()
    pl.when(p == 2)(up3.wait_send)
    pl.when(p == 1)(down3.wait_send)


def behind(normed, metas, wts):
    d = normed.shape[1]
    width = d // CHUNKS
    slots = PLANE * 4 * CAP
    units = SUB * 96
    dma = lambda *shape: pltpu.SemaphoreType.DMA(shape)
    return pl.pallas_call(
        back_kernel,
        out_shape=jax.ShapeDtypeStruct((64, d), jnp.bfloat16),
        in_specs=[VMEM, VMEM, ANY],
        out_specs=VMEM,
        scratch_shapes=[
            pltpu.VMEM((3, units, d), jnp.bfloat16),
            pltpu.VMEM((slots, 256), jnp.bfloat16),
            pltpu.VMEM((slots, 256), jnp.bfloat16),
            pltpu.VMEM((CHUNKS, 256, width), jnp.bfloat16),
            pltpu.VMEM((CHUNKS, slots, width), jnp.bfloat16),
            pltpu.VMEM((CHUNKS, slots, width), jnp.bfloat16),
            pltpu.VMEM((2, slots, units), jnp.float32),
            pltpu.VMEM((slots, units), jnp.bfloat16),
            pltpu.VMEM((CHUNKS, slots, width), jnp.bfloat16),
            pltpu.VMEM((CHUNKS, slots, width), jnp.bfloat16),
            pltpu.VMEM((CHUNKS, 256, width), jnp.float32),
            pltpu.VMEM((CHUNKS, 3, 64, width), jnp.bfloat16),
            pltpu.VMEM((CHUNKS, 3, 64, width), jnp.bfloat16),
            dma(CHUNKS, 2), dma(CHUNKS, 2), dma(CHUNKS, 2), dma(CHUNKS, 2),
            dma(CHUNKS), dma(CHUNKS), dma(CHUNKS), dma(CHUNKS),
            dma(CHUNKS, 2), dma(CHUNKS, 2), dma(CHUNKS, 2), dma(CHUNKS, 2),
            dma(2), dma(2), dma(SUB), dma(2),
        ],
        compiler_params=pltpu.CompilerParams(
            collective_id=1, has_side_effects=True, vmem_limit_bytes=52 * 2**20
        ),
        cost_estimate=pl.CostEstimate(flops=6 * 10**9, bytes_accessed=10**7, transcendentals=10**6),
    )(normed, metas, wts)


def routing(ids, keep, logits):
    experts = logits.shape[1]
    hit = ids[:, :, None] == jnp.arange(experts, dtype=jnp.int32)
    named = jnp.any(hit, axis=1)
    kept = jnp.any(hit & (keep[:, :, None] == 1), axis=1)
    tokens = ids.shape[0]
    earlier = jnp.tril(jnp.ones((tokens, tokens), jnp.bfloat16), -1)
    before = jnp.dot(earlier, kept.astype(jnp.bfloat16), preferred_element_type=jnp.float32)
    slot = jnp.where(kept, before, -1.0)
    chosen = jnp.where(named, logits, -jnp.inf)
    terms = jnp.exp(chosen - jnp.max(chosen, axis=-1, keepdims=True))
    probs = terms / jnp.sum(terms, axis=-1, keepdims=True)
    weight = jnp.where(kept, probs, 0.0)
    both = jnp.stack([slot, weight])
    both = jnp.transpose(both, (0, 2, 1)).reshape(2, X, 2, Y * CORES, tokens)
    both = jnp.transpose(both, (2, 0, 1, 3, 4)).reshape(2, 2 * PLANE, tokens)
    return jnp.concatenate([both, both], axis=-1)


def shards(
    queries, key_heads, value_heads, doc_ids, residual, w_out, norm_gain, router_logits, expert_ids, keep_mask,
    w_gate, w_up, w_down,
):
    s = lax.axis_index("seq")
    doc = jnp.pad(doc_ids[0], (256, 0), constant_values=-1)
    span = lax.dynamic_slice(doc, (64 * s,), (320,))
    causal = jnp.arange(320)[None, :] <= 256 + jnp.arange(64)[:, None]
    bias = jnp.where(causal & (span[None, :] == span[256:, None]), 0.0, NEG).astype(jnp.float32)
    meta = routing(expert_ids[0], keep_mask[0], router_logits[0])
    hidden, normed, wts, metas = front(
        queries[0], key_heads[0], value_heads[0], bias, residual[0], norm_gain[None], meta, w_out,
        w_gate[0], w_up[0], w_down[0],
    )
    return hidden[None], behind(normed, metas, wts)[None]


def solution(mesh):
    split = P("exp", "seq", None)
    return jax.shard_map(
        shards,
        mesh=mesh,
        in_specs=(split, split, split, P("exp", None), split, P("seq", None), P()) + (split,) * 6,
        out_specs=(split, split),
        check_vma=False,
    )
```

time: 625 us -> 328 us (0.52)
  the two profiles are of different devices: /device:TPU:97 before, /device:TPU:57 now
where the time goes in v1:
time: 328 us
  Pallas kernels  311 us (95%)
  local copies, waits for them, and re-layouts  12.1 us (4%)
  other arithmetic  3.8 us (1%)
    pallas_call x1, Pallas kernels, behind(): pl.pallas_call(back_kernel, out_shape=jax.ShapeDtypeStruct((64, d), jnp.b...  192 us
    pallas_call x1, Pallas kernels, front(): pl.pallas_call(front_kernel, out_shape=(jax.ShapeDtypeStruct((64, d), jnp...  118 us
    unnamed x20, local copies, waits for them, and re-layouts  10.3 us

profile of v1, /device:TPU:57, one launch (start us, length us, event | category | flops | bytes accessed | tf_op | source)
XLA Modules:
  0.0 327.5 jit_solution(903518760141891312)
XLA Ops:
  0.7 0.7 compare_bitcast_fusion
  1.3 0.8 pad_dynamic-slice_fusion
  2.1 0.1 copy.23
  2.2 0.8 copy.22
  3.0 0.3 fusion.3
  3.2 0.9 fusion.7
  4.1 1.0 exponential_reduce_fusion
  5.1 0.9 divide_select_fusion
  5.9 0.2 fusion
  6.2 0.1 pad_maximum_fusion.meta_ref
  6.3 0.1 fusion.5.bias_ref
  6.4 1.6 copy-done
  8.0 1.0 copy-done.1
  9.1 1.0 copy-done.2
  10.1 1.0 copy-done.3
  11.1 1.0 copy-done.4
  12.0 0.9 copy-done.5
  13.0 0.8 copy-done.6
  13.8 0.8 copy-done.7
  14.7 0.7 copy-done.8
  15.4 118.3 %shard_map.140 = (bf16[64,2048]{1,0:T(8,128)(2,1)S(1)}, bf16[64,2048]{1,0:T(8,128)(2,1)S(1)}, bf16[3,384,2048]{2,1,0:T(8,128)(2,1)}, f32[4,64,128]{2,1,0:T(8,128)S(1)}) custom-call(bf16[64,4096]{1,0:T(8,128)(2,1)S(1)} %bitcast.33, bf16[64,512]{1,0:T(8,128)(2,1)S(1)} %bitcast.40, bf16[64,512]{1,0:T(8,128)(2,1)S(1)} %bitcast.41, ...), custom_call_target="tpu_custom_call" | custom-call | flops 1000000000 | bytes 20000000 | tf_op jit(solution)/shard_map/pallas_call | solution.py:234
  133.6 192.5 %shard_map.141 = bf16[64,2048]{1,0:T(8,128)(2,1)S(1)} custom-call(bf16[64,2048]{1,0:T(8,128)(2,1)S(1)} %get-tuple-element.7.normed_ref, f32[4,64,128]{2,1,0:T(8,128)S(1)} %get-tuple-element.8.metas_ref, bf16[3,384,2048]{2,1,0:T(8,128)(2,1)} %get-tuple-element.9.wts_ref), custom_call_target="tpu_custom_call" | custom-call | flops 6000000000 | bytes 10000000 | tf_op jit(solution)/shard_map/pallas_call | solution.py:490
  326.1 0.7 copy.28
  326.8 0.7 copy.29
  (15 shorter events, 0.1 us)
Async XLA Ops:
  6.4 1.6 copy-start
  8.0 1.0 copy-start.1
  9.1 1.0 copy-start.2
  10.1 1.0 copy-start.3
  11.0 1.0 copy-start.4
  12.0 0.9 copy-start.5
  13.0 0.8 copy-start.6
  13.8 0.8 copy-start.7
  14.7 0.7 copy-start.8

commit v2 on v1

v2 whole, which is shorter than its diff:
```python
import jax
import jax.numpy as jnp
from jax import lax
from jax.experimental import pallas as pl
from jax.experimental.pallas import tpu as pltpu
from jax.sharding import PartitionSpec as P

MESH = pl.DeviceIdType.MESH
HD = 128
CAP = 8
X, Y, Z, LINE, CORES = 4, 4, 16, 8, 2
PLANE = X * Y * CORES
SUB = 4
CHUNKS = 4
EPSILON = 1e-06
NEG = -1e30
ANY = pl.BlockSpec(memory_space=pl.ANY)
VMEM = pl.BlockSpec(memory_space=pltpu.VMEM)
Z_OFFSETS = (1, -1, 2, -2, 3, -3, 4)


def place():
    s = lax.axis_index("seq")
    e = lax.axis_index("exp")
    c = e % 2
    y = (e // 2) % Y
    zh = (e // (2 * Y)) % 2
    x = e // (4 * Y)
    return x, y, zh * LINE + s, c


def device(x, y, z, c):
    x, y, z = x % X, y % Y, z % Z
    return {"seq": z % LINE, "exp": ((x * 2 + z // LINE) * Y + y) * 2 + c}


def rows(start, count):
    return pl.ds(pl.multiple_of(start, 16), count)


def layer_kernel(
    q_hbm, k_hbm, v_hbm, span_hbm, res_hbm, gain_hbm, logits_hbm, ids_hbm, keep_hbm, wout_ref, wg_ref, wu_ref, wd_ref,
    hidden_ref, out_ref,
    q_ref, kv, span_ref, res_ref, gain_ref, logits_ref, ids_ref, keep_ref, meta, metas,
    wbuf, att, total, wv, pick, comb, tok, sent, got, accum, act, made, back, part, far, home,
    send, recv, local,
    z_send, z_recv, h_send, h_recv, p_send, p_recv, r_send, r_recv, f_send, f_recv, o_send, o_recv,
):
    x, y, z, c = place()
    s = z % LINE
    zh = z // LINE
    p = z % SUB
    me = (x * Y + y) * CORES + c
    width = tok.shape[2]

    def at(dx=0, dy=0, dz=0):
        return device(x + dx + X, y + dy + Y, z + dz + Z, c)

    def partner(o):
        dx = o % X
        px = (x + dx) % X
        py = (y + o // (X * CORES) + dx) % Y
        pc = (c + o // X) % CORES
        return (px * Y + py) * CORES + pc, device(px, py, z, pc)

    sibling = device(x, y, z, 1 - c)
    counter = [0]

    def remote(src, dst, peer):
        i = counter[0]
        counter[0] += 1
        return copy_to(src, dst, send.at[i], recv.at[i], peer)

    def copy_to(src, dst, ss, rs, peer):
        return pltpu.make_async_remote_copy(
            src_ref=src, dst_ref=dst, send_sem=ss, recv_sem=rs, device_id=peer, device_id_type=MESH
        )

    def block(owner):
        return wv.at[:, rows(96 * ((owner + SUB) % SUB), 96)]

    ja = (y * 2 + c) * X + x
    jb = (x * 2 + c) * Y + y
    mine = jnp.where(s < 4, ja, jb) * 16
    piece = wbuf.at[s, rows(mine, 16)]
    moves = [
        (k_hbm, kv.at[4, 0]), (v_hbm, kv.at[4, 1]), (wout_ref.at[rows(mine, 16)], piece),
        (ids_hbm, ids_ref), (keep_hbm, keep_ref), (logits_hbm, logits_ref), (span_hbm, span_ref),
        (wg_ref, wv.at[0, rows(96 * p, 96)]), (wu_ref, wv.at[1, rows(96 * p, 96)]),
        (wd_ref, wv.at[2, rows(96 * p, 96)]),
        (q_hbm, q_ref), (res_hbm, res_ref), (gain_hbm, gain_ref),
    ]
    loads = [pltpu.make_async_copy(src, dst, local.at[i]) for i, (src, dst) in enumerate(moves)]
    for load in loads:
        load.start()

    barrier = pltpu.get_barrier_semaphore()
    for d in (1, -1, 2, -2, 3, -3, 4, -4, 8):
        pl.semaphore_signal(barrier, inc=1, device_id=at(dz=d), device_id_type=MESH)

    def greet(o, _):
        pl.semaphore_signal(barrier, inc=1, device_id=partner(o)[1], device_id_type=MESH)
        return 0

    lax.fori_loop(1, PLANE, greet, 0)
    pl.semaphore_wait(barrier, 9 + PLANE - 1)

    kv_steps = [remote(kv.at[4 - d], kv.at[3 - d], at(dz=1)) for d in range(4)]
    z_copies = [remote(piece, piece, at(dz=d)) for d in Z_OFFSETS]
    for load in loads[:3]:
        load.wait()
    for copy in z_copies:
        copy.start()
    kv_steps[0].start()

    for load in loads[3:7]:
        load.wait()
    experts = logits_ref.shape[1]
    expert = lax.broadcasted_iota(jnp.int32, (experts, 64), 0)
    named = expert == ids_ref[0:1, :]
    kept = named & (keep_ref[0:1, :] == 1)
    for k in range(1, ids_ref.shape[0]):
        hit = expert == ids_ref[k:k + 1, :]
        named = named | hit
        kept = kept | (hit & (keep_ref[k:k + 1, :] == 1))
    earlier = lax.broadcasted_iota(jnp.int32, (64, 64), 0) < lax.broadcasted_iota(jnp.int32, (64, 64), 1)
    before = jnp.dot(
        jnp.where(kept, 1.0, 0.0).astype(jnp.bfloat16),
        jnp.where(earlier, 1.0, 0.0).astype(jnp.bfloat16),
        preferred_element_type=jnp.float32,
    )
    slot = jnp.where(kept, before, -1.0)
    chosen = jnp.where(named, logits_ref[...], -jnp.inf)
    terms = jnp.exp(chosen - jnp.max(chosen, axis=0, keepdims=True))
    weight = jnp.where(kept, terms / jnp.sum(terms, axis=0, keepdims=True), 0.0)
    slot = jnp.concatenate([slot, slot], axis=1)
    weight = jnp.concatenate([weight, weight], axis=1)
    group = Y * CORES
    for half in range(2):
        for i in range(X):
            chunk = slice(group * (2 * i + half), group * (2 * i + half + 1))
            meta[half, group * i:group * (i + 1)] = slot[chunk]
            meta[half, PLANE + group * i:PLANE + group * (i + 1)] = weight[chunk]
    metas[0] = meta[zh]
    meta_copies = [
        remote(meta.at[1 - zh], metas.at[3], at(dz=8)),
        remote(meta.at[((z + 4) % Z) // LINE], metas.at[1], at(dz=4)),
        remote(meta.at[((z + 12) % Z) // LINE], metas.at[2], at(dz=-4)),
    ]
    for copy in meta_copies:
        copy.start()

    kv_steps[0].wait_recv()
    kv_steps[1].start()
    for copy in z_copies:
        copy.wait_recv()

    up1 = remote(block(p), block(p), at(dz=1))
    down1 = remote(block(p), block(p), at(dz=-1))
    up2 = remote(block(p - 1), block(p - 1), at(dz=1))
    down2 = remote(block(p + 1), block(p + 1), at(dz=-1))
    up3 = remote(block(0), block(0), at(dz=1))
    down3 = remote(block(3), block(3), at(dz=-1))

    def ring(region, lo, step):
        first = [remote(region(0, lo, 4), region(0, lo, 4), step(d)) for d in (1, -1)]
        second = [
            remote(region(-1, lo, 2), region(-1, lo, 2), step(1)),
            remote(region(1, lo + 2, 2), region(1, lo + 2, 2), step(-1)),
        ]
        return first, second

    def region_ax(d, lo, n):
        return wbuf.at[pl.ds(lo, n), rows(16 * ((y * 2 + c) * X + (x + d + X) % X), 16)]

    def region_by(d, lo, n):
        return wbuf.at[pl.ds(lo, n), rows(16 * ((x * 2 + c) * Y + (y + d + Y) % Y), 16)]

    def region_ay(d, lo, n):
        return wbuf.at[pl.ds(lo, n), rows(64 * (((y + d + Y) % Y) * 2 + c), 64)]

    def region_bx(d, lo, n):
        return wbuf.at[pl.ds(lo, n), rows(64 * (((x + d + X) % X) * 2 + c), 64)]

    step_x = lambda d: at(dx=d)
    step_y = lambda d: at(dy=d)
    a1, a2 = ring(region_ax, 0, step_x)
    b1, b2 = ring(region_by, 4, step_y)
    for copy in a1 + b1:
        copy.start()
    for load in loads[7:10]:
        load.wait()
    pl.when(p < 3)(up1.start)
    pl.when(p > 0)(down1.start)
    kv_steps[1].wait_recv()
    kv_steps[2].start()
    for copy in a1 + b1:
        copy.wait_recv()
    for copy in a2 + b2:
        copy.start()
    kv_steps[2].wait_recv()
    kv_steps[3].start()
    for copy in a2 + b2:
        copy.wait_recv()
    c1, c2 = ring(region_ay, 0, step_y)
    d1, d2 = ring(region_bx, 4, step_x)
    twins = {
        d: [
            remote(region_ay(d, 0, 4), region_ay(d, 0, 4), sibling),
            remote(region_bx(d, 4, 4), region_bx(d, 4, 4), sibling),
        ]
        for d in (0, 1, -1, 2)
    }
    for copy in c1 + d1 + twins[0]:
        copy.start()

    for copy in meta_copies:
        copy.wait_recv()
    for a in range(2):
        lane = lax.broadcasted_iota(jnp.int32, (PLANE, 128), 1)
        slots = jnp.where(lane < 64, metas[2 * a, 0:PLANE], metas[2 * a + 1, 0:PLANE])
        weights = jnp.where(lane < 64, metas[2 * a, PLANE:], metas[2 * a + 1, PLANE:])
        row = lax.broadcasted_iota(jnp.int32, (PLANE, 4 * CAP, 128), 1)
        column = lax.broadcasted_iota(jnp.int32, (PLANE, 4 * CAP, 128), 2)
        same = row // CAP == 2 * a + column // 64
        hit = same & (slots[:, None, :] == (row % CAP).astype(jnp.float32))
        pick[:, 128 * a:128 * (a + 1)] = (
            jnp.where(hit, 1.0, 0.0).reshape(PLANE * 4 * CAP, 128).astype(jnp.bfloat16)
        )
        comb[:, 128 * a:128 * (a + 1)] = (
            jnp.where(hit, weights[:, None, :], 0.0).reshape(PLANE * 4 * CAP, 128).astype(jnp.bfloat16)
        )

    docs = lax.broadcasted_iota(jnp.int32, (8, 320), 0)
    key_doc = jnp.where(docs == span_ref[...], 1.0, 0.0).astype(jnp.bfloat16)
    same_doc = lax.dot_general(
        key_doc[:, 256:320], key_doc, (((0,), (0,)), ((), ())), preferred_element_type=jnp.float32
    )
    key_at = lax.broadcasted_iota(jnp.int32, (64, 320), 1)
    query_at = lax.broadcasted_iota(jnp.int32, (64, 320), 0)
    bias = jnp.where((key_at <= query_at + 256) & (same_doc > 0.5), 0.0, NEG)
    loads[10].wait()
    kv_steps[3].wait_recv()
    for g in range(4):
        head = lambda h: (g * 8 + h) * HD
        queries = jnp.concatenate([q_ref[:, head(h):head(h) + HD] for h in range(8)], axis=0)
        keys = kv[:, 0, :, g * HD:(g + 1) * HD].reshape(5 * 64, HD)
        values = kv[:, 1, :, g * HD:(g + 1) * HD].reshape(5 * 64, HD)
        scores = lax.dot_general(
            queries, keys, (((1,), (1,)), ((), ())), preferred_element_type=jnp.float32
        ) * (1.0 / HD**0.5)
        scores = (scores.reshape(8, 64, 320) + bias[None]).reshape(512, 320)
        terms = jnp.exp(scores - jnp.max(scores, axis=-1, keepdims=True))
        probs = (terms / jnp.sum(terms, axis=-1, keepdims=True)).astype(jnp.bfloat16)
        out = jnp.dot(probs, values, preferred_element_type=jnp.float32).astype(jnp.bfloat16)
        for h in range(8):
            att[:, head(h):head(h) + HD] = out[64 * h:64 * (h + 1)]

    pl.when(p > 0)(up1.wait_recv)
    pl.when(p < 3)(down1.wait_recv)
    pl.when((p > 0) & (p < 3))(up2.start)
    pl.when((p > 0) & (p < 3))(down2.start)
    for copy in c1 + d1:
        copy.wait_recv()
    for copy in c2 + d2 + twins[1] + twins[-1]:
        copy.start()
    for copy in c2 + d2:
        copy.wait_recv()
    for copy in twins[2]:
        copy.start()
    pl.when(p > 1)(up2.wait_recv)
    pl.when(p < 2)(down2.wait_recv)
    pl.when(p == 2)(up3.start)
    pl.when(p == 1)(down3.start)
    for d in (0, 1, -1, 2):
        for copy in twins[d]:
            copy.wait_recv()

    for load in loads[11:]:
        load.wait()
    for n in range(4):
        cols = slice(512 * n, 512 * (n + 1))
        acc = res_ref[:, cols].astype(jnp.float32)
        for t in range(8):
            acc = acc + jnp.dot(
                att[:, 512 * t:512 * (t + 1)], wbuf[t, :, cols], preferred_element_type=jnp.float32
            )
        total[:, cols] = acc
    hidden = total[...]
    square = jnp.mean(hidden * hidden, axis=-1, keepdims=True)
    normed = (hidden * lax.rsqrt(square + EPSILON) * gain_ref[...]).astype(jnp.bfloat16)
    for q in range(CHUNKS):
        tok[q, 0:64] = normed[:, width * q:width * (q + 1)]

    near = [
        (
            copy_to(tok.at[q, pl.ds(0, 64)], tok.at[q, pl.ds(64, 64)], z_send.at[q, 0], z_recv.at[q, 0], at(dz=4)),
            copy_to(tok.at[q, pl.ds(0, 64)], tok.at[q, pl.ds(128, 64)], z_send.at[q, 1], z_recv.at[q, 1], at(dz=-4)),
        )
        for q in range(CHUNKS)
    ]
    across = [
        (
            copy_to(tok.at[q, pl.ds(64, 32)], tok.at[q, pl.ds(192, 32)], h_send.at[q, 0], h_recv.at[q, 0], at(dz=4)),
            copy_to(tok.at[q, pl.ds(160, 32)], tok.at[q, pl.ds(224, 32)], h_send.at[q, 1], h_recv.at[q, 1], at(dz=-4)),
        )
        for q in range(CHUNKS)
    ]
    for q in range(CHUNKS):
        for copy in near[q]:
            copy.start()
    hidden_ref[...] = hidden.astype(jnp.bfloat16)

    def spread(src, dst, q, ss, rs):
        def go(o, _):
            peer, where = partner(o)
            copy_to(
                src.at[q, rows(32 * peer, 32)], dst.at[q, rows(32 * me, 32)], ss.at[q], rs.at[q], where
            ).start()
            return 0

        lax.fori_loop(1, PLANE, go, 0)
        dst[q, rows(32 * me, 32)] = src[q, rows(32 * me, 32)]

    def whole(src, dst, q, ss, rs):
        every = pl.ds(0, 32 * (PLANE - 1))
        return copy_to(src.at[q, every], dst.at[q, every], ss.at[q], rs.at[q], at(dz=1))

    def dispatch(q):
        for copy in across[q]:
            copy.wait_recv()

        def tile(i, _):
            part_rows = pl.ds(pl.multiple_of(i * 256, 256), 256)
            sent[q, part_rows] = jnp.dot(
                pick[part_rows], tok[q], preferred_element_type=jnp.float32
            ).astype(jnp.bfloat16)
            return 0

        lax.fori_loop(0, 4, tile, 0)
        spread(sent, got, q, p_send, p_recv)

    for q in range(CHUNKS):
        for copy in near[q]:
            copy.wait_recv()
        for copy in across[q]:
            copy.start()
        if q >= 1:
            dispatch(q - 1)
    dispatch(CHUNKS - 1)

    pl.when(p == 3)(up3.wait_recv)
    pl.when(p == 0)(down3.wait_recv)
    transposed = (((1,), (1,)), ((), ()))
    for q in range(CHUNKS):
        whole(sent, got, q, p_send, p_recv).wait_recv()
        cols = slice(width * q, width * (q + 1))

        def tile(i, _, q=q, cols=cols):
            part_rows = pl.ds(pl.multiple_of(i * 256, 256), 256)
            for m in range(2):
                value = lax.dot_general(
                    got[q, part_rows], wv[m, :, cols], transposed, preferred_element_type=jnp.float32
                )
                if q == 0:
                    accum[m, part_rows] = value
                else:
                    accum[m, part_rows] += value
            return 0

        lax.fori_loop(0, 4, tile, 0)

    def activate(i, _):
        part_rows = pl.ds(pl.multiple_of(i * 256, 256), 256)
        gate = accum[0, part_rows]
        act[part_rows] = (gate / (1.0 + jnp.exp(-gate)) * accum[1, part_rows]).astype(jnp.bfloat16)
        return 0

    lax.fori_loop(0, 4, activate, 0)

    for q in range(CHUNKS):
        cols = slice(width * q, width * (q + 1))

        def tile(i, _, q=q, cols=cols):
            part_rows = pl.ds(pl.multiple_of(i * 256, 256), 256)
            made[q, part_rows] = jnp.dot(
                act[part_rows], wv[2, :, cols], preferred_element_type=jnp.float32
            ).astype(jnp.bfloat16)
            return 0

        lax.fori_loop(0, 4, tile, 0)
        spread(made, back, q, r_send, r_recv)

    def half_copies(q):
        return (
            copy_to(far.at[q, 0, pl.ds(0, 32)], home.at[q, 0, pl.ds(0, 32)], f_send.at[q, 0], f_recv.at[q, 0], at(dz=4)),
            copy_to(far.at[q, 0, pl.ds(32, 32)], home.at[q, 0, pl.ds(32, 32)], f_send.at[q, 1], f_recv.at[q, 1], at(dz=-4)),
        )

    def home_copies(q):
        return (
            copy_to(far.at[q, 1], home.at[q, 1], o_send.at[q, 0], o_recv.at[q, 0], at(dz=-4)),
            copy_to(far.at[q, 2], home.at[q, 2], o_send.at[q, 1], o_recv.at[q, 1], at(dz=4)),
        )

    def combine(q):
        whole(made, back, q, r_send, r_recv).wait_recv()
        part[q] = lax.dot_general(
            comb[...], back[q], (((0,), (0,)), ((), ())), preferred_element_type=jnp.float32
        )
        far[q, 0] = part[q, 192:256].astype(jnp.bfloat16)
        for copy in half_copies(q):
            copy.start()

    def relay(q):
        for copy in half_copies(q):
            copy.wait_recv()
        ahead, behind = part[q, 128:192], part[q, 64:128]
        far[q, 2, 0:32] = (ahead[0:32] + home[q, 0, 0:32].astype(jnp.float32)).astype(jnp.bfloat16)
        far[q, 2, 32:64] = ahead[32:64].astype(jnp.bfloat16)
        far[q, 1, 0:32] = behind[0:32].astype(jnp.bfloat16)
        far[q, 1, 32:64] = (behind[32:64] + home[q, 0, 32:64].astype(jnp.float32)).astype(jnp.bfloat16)
        for copy in home_copies(q):
            copy.start()

    def finish(q):
        for copy in home_copies(q):
            copy.wait_recv()
        total = part[q, 0:64] + home[q, 1].astype(jnp.float32) + home[q, 2].astype(jnp.float32)
        out_ref[:, width * q:width * (q + 1)] = total.astype(jnp.bfloat16)

    for step in range(CHUNKS + 2):
        if step < CHUNKS:
            combine(step)
        if 0 <= step - 1 < CHUNKS:
            relay(step - 1)
        if 0 <= step - 2 < CHUNKS:
            finish(step - 2)

    for q in range(CHUNKS):
        for copy in near[q] + across[q] + half_copies(q) + home_copies(q):
            copy.wait_send()
        whole(sent, got, q, p_send, p_recv).wait_send()
        whole(made, back, q, r_send, r_recv).wait_send()
    for copy in kv_steps + z_copies + meta_copies + a1 + b1 + a2 + b2 + c1 + d1 + c2 + d2:
        copy.wait_send()
    for d in (0, 1, -1, 2):
        for copy in twins[d]:
            copy.wait_send()
    pl.when(p < 3)(up1.wait_send)
    pl.when(p > 0)(down1.wait_send)
    pl.when((p > 0) & (p < 3))(up2.wait_send)
    pl.when((p > 0) & (p < 3))(down2.wait_send)
    pl.when(p == 2)(up3.wait_send)
    pl.when(p == 1)(down3.wait_send)


def layer(*args):
    d = args[4].shape[1]
    width = d // CHUNKS
    slots = PLANE * 4 * CAP
    units = SUB * 96
    dma = lambda *shape: pltpu.SemaphoreType.DMA(shape)
    half = lambda *shape: pltpu.VMEM(shape, jnp.bfloat16)
    full = lambda *shape: pltpu.VMEM(shape, jnp.float32)
    return pl.pallas_call(
        layer_kernel,
        out_shape=(jax.ShapeDtypeStruct((64, d), jnp.bfloat16), jax.ShapeDtypeStruct((64, d), jnp.bfloat16)),
        in_specs=[ANY] * len(args),
        out_specs=(VMEM, VMEM),
        scratch_shapes=[
            half(64, 4096), half(5, 2, 64, 512), pltpu.VMEM((1, 320), jnp.int32), half(64, d), full(1, d),
            full(64, 64), pltpu.VMEM((8, 64), jnp.int32), pltpu.VMEM((8, 64), jnp.int32),
            full(2, 64, 128), full(4, 64, 128),
            half(LINE, 512, d), half(64, 4096), full(64, d), half(3, units, d),
            half(slots, 256), half(slots, 256), half(CHUNKS, 256, width),
            half(CHUNKS, slots, width), half(CHUNKS, slots, width),
            full(2, slots, units), half(slots, units),
            half(CHUNKS, slots, width), half(CHUNKS, slots, width),
            full(CHUNKS, 256, width), half(CHUNKS, 3, 64, width), half(CHUNKS, 3, 64, width),
            dma(48), dma(48), dma(13),
            dma(CHUNKS, 2), dma(CHUNKS, 2), dma(CHUNKS, 2), dma(CHUNKS, 2),
            dma(CHUNKS), dma(CHUNKS), dma(CHUNKS), dma(CHUNKS),
            dma(CHUNKS, 2), dma(CHUNKS, 2), dma(CHUNKS, 2), dma(CHUNKS, 2),
        ],
        compiler_params=pltpu.CompilerParams(
            collective_id=0, has_side_effects=True, vmem_limit_bytes=60 * 2**20
        ),
        cost_estimate=pl.CostEstimate(flops=7 * 10**9, bytes_accessed=3 * 10**7, transcendentals=10**6),
    )(*args)


def shards(
    queries, key_heads, value_heads, doc_ids, residual, w_out, norm_gain, router_logits, expert_ids, keep_mask,
    w_gate, w_up, w_down,
):
    s = lax.axis_index("seq")
    doc = jnp.pad(doc_ids[0], (256, 0), constant_values=-1)
    span = lax.dynamic_slice(doc, (64 * s,), (320,))[None]
    hidden, out = layer(
        queries[0], key_heads[0], value_heads[0], span, residual[0], norm_gain[None], router_logits[0].T,
        expert_ids[0].T, keep_mask[0].T, w_out, w_gate[0], w_up[0], w_down[0],
    )
    return hidden[None], out[None]


def solution(mesh):
    split = P("exp", "seq", None)
    return jax.shard_map(
        shards,
        mesh=mesh,
        in_specs=(split, split, split, P("exp", None), split, P("seq", None), P()) + (split,) * 6,
        out_specs=(split, split),
        check_vma=False,
    )
```

time: 328 us -> 289 us (0.88)
  the two profiles are of different devices: /device:TPU:57 before, /device:TPU:48 now
where the time goes in v2:
time: 289 us
  Pallas kernels  282 us (98%)
  local copies, waits for them, and re-layouts  6.12 us (2%)
    pallas_call x1, Pallas kernels, layer(): pl.pallas_call(layer_kernel, out_shape=(jax.ShapeDtypeStruct((64, d), jnp...  282 us

profile of v2, /device:TPU:48, one launch (start us, length us, event | category | flops | bytes accessed | tf_op | source)
XLA Modules:
  0.0 289.1 jit_solution(8174646495254092131)
XLA Ops:
  0.6 0.8 pad_dynamic-slice_fusion
  1.4 0.6 broadcast_in_dim.12.span_hbm
  2.0 1.5 copy.15
  3.4 282.3 %shard_map.140 = (bf16[64,2048]{1,0:T(8,128)(2,1)}, bf16[64,2048]{1,0:T(8,128)(2,1)}) custom-call(bf16[64,4096]{1,0:T(8,128)(2,1)} %bitcast.24, bf16[64,512]{1,0:T(8,128)(2,1)} %bitcast.29, bf16[64,512]{1,0:T(8,128)(2,1)} %bitcast.30, s32[1,320]{1,0:T(1,128)} %broadcast_in_dim.12.span_hbm, bf16[64,2048]{1,0:T(8,128)(2,1)} %bitcast.28, f32[1,2048]{1,0:T(1,128)} %bitcast.31, ...), custom_call_target="tpu_custom_call" | custom-call | flops 7000000000 | bytes 30000000 | tf_op jit(solution)/shard_map/pallas_call | solution.py:466
  285.8 1.7 copy.18
  287.4 1.7 copy.19

commit v3 on v2

--- a/solution.py
+++ b/solution.py
@@ -150,10 +150,10 @@
     for copy in meta_copies:
         copy.start()
 
+    for copy in z_copies:
+        copy.wait_recv()
     kv_steps[0].wait_recv()
     kv_steps[1].start()
-    for copy in z_copies:
-        copy.wait_recv()
 
     up1 = remote(block(p), block(p), at(dz=1))
     down1 = remote(block(p), block(p), at(dz=-1))
@@ -162,57 +162,58 @@
     up3 = remote(block(0), block(0), at(dz=1))
     down3 = remote(block(3), block(3), at(dz=-1))
 
-    def ring(region, lo, step):
-        first = [remote(region(0, lo, 4), region(0, lo, 4), step(d)) for d in (1, -1)]
+    def piece_a(dx, dy, lo, n):
+        return wbuf.at[pl.ds(lo, n), rows(16 * ((((y + dy + Y) % Y) * 2 + c) * X + (x + dx + X) % X), 16)]
+
+    def piece_b(dx, dy, lo, n):
+        return wbuf.at[pl.ds(4 + lo, n), rows(16 * ((((x + dx + X) % X) * 2 + c) * Y + (y + dy + Y) % Y), 16)]
+
+    def lap(region, step):
+        first = [remote(region(0, 0, 4), region(0, 0, 4), step(d)) for d in (1, -1)]
         second = [
-            remote(region(-1, lo, 2), region(-1, lo, 2), step(1)),
-            remote(region(1, lo + 2, 2), region(1, lo + 2, 2), step(-1)),
+            remote(region(-1, 0, 2), region(-1, 0, 2), step(1)),
+            remote(region(1, 2, 2), region(1, 2, 2), step(-1)),
         ]
         return first, second
 
-    def region_ax(d, lo, n):
-        return wbuf.at[pl.ds(lo, n), rows(16 * ((y * 2 + c) * X + (x + d + X) % X), 16)]
-
-    def region_by(d, lo, n):
-        return wbuf.at[pl.ds(lo, n), rows(16 * ((x * 2 + c) * Y + (y + d + Y) % Y), 16)]
-
-    def region_ay(d, lo, n):
-        return wbuf.at[pl.ds(lo, n), rows(64 * (((y + d + Y) % Y) * 2 + c), 64)]
-
-    def region_bx(d, lo, n):
-        return wbuf.at[pl.ds(lo, n), rows(64 * (((x + d + X) % X) * 2 + c), 64)]
-
     step_x = lambda d: at(dx=d)
     step_y = lambda d: at(dy=d)
-    a1, a2 = ring(region_ax, 0, step_x)
-    b1, b2 = ring(region_by, 4, step_y)
-    for copy in a1 + b1:
+    a1, a2 = lap(lambda d, lo, n: piece_a(d, 0, lo, n), step_x)
+    b1, b2 = lap(lambda d, lo, n: piece_b(0, d, lo, n), step_y)
+    second_a = {o: lap(lambda d, lo, n, o=o: piece_a(o, d, lo, n), step_y) for o in (0, 1, -1, 2)}
+    second_b = {o: lap(lambda d, lo, n, o=o: piece_b(d, o, lo, n), step_x) for o in (0, 1, -1, 2)}
+    c1 = {o: second_a[o][0] + second_b[o][0] for o in second_a}
+    c2 = {o: second_a[o][1] + second_b[o][1] for o in second_a}
+
+    def lane_a(d):
+        return wbuf.at[pl.ds(0, 4), rows(64 * (((y + d + Y) % Y) * 2 + c), 64)]
+
+    def lane_b(d):
+        return wbuf.at[pl.ds(4, 4), rows(64 * (((x + d + X) % X) * 2 + c), 64)]
+
+    twins = {d: [remote(lane_a(d), lane_a(d), sibling), remote(lane_b(d), lane_b(d), sibling)] for d in (0, 1, -1, 2)}
+    for copy in a1 + b1 + c1[0]:
         copy.start()
     for load in loads[7:10]:
         load.wait()
     pl.when(p < 3)(up1.start)
     pl.when(p > 0)(down1.start)
+    for copy in a1 + b1:
+        copy.wait_recv()
+    for copy in a2 + b2 + c1[1] + c1[-1]:
+        copy.start()
     kv_steps[1].wait_recv()
     kv_steps[2].start()
-    for copy in a1 + b1:
-        copy.wait_recv()
+    for copy in c1[0]:
+        copy.wait_recv()
+    for copy in c2[0]:
+        copy.start()
     for copy in a2 + b2:
+        copy.wait_recv()
+    for copy in c1[2] + twins[0]:
         copy.start()
     kv_steps[2].wait_recv()
     kv_steps[3].start()
-    for copy in a2 + b2:
-        copy.wait_recv()
-    c1, c2 = ring(region_ay, 0, step_y)
-    d1, d2 = ring(region_bx, 4, step_x)
-    twins = {
-        d: [
-            remote(region_ay(d, 0, 4), region_ay(d, 0, 4), sibling),
-            remote(region_bx(d, 4, 4), region_bx(d, 4, 4), sibling),
-        ]
-        for d in (0, 1, -1, 2)
-    }
-    for copy in c1 + d1 + twins[0]:
-        copy.start()
 
     for copy in meta_copies:
         copy.wait_recv()
@@ -256,22 +257,23 @@
         for h in range(8):
             att[:, head(h):head(h) + HD] = out[64 * h:64 * (h + 1)]
 
+    for copy in c1[1] + c1[-1]:
+        copy.wait_recv()
+    for copy in c2[1] + c2[-1]:
+        copy.start()
+    for copy in c1[2]:
+        copy.wait_recv()
+    for copy in c2[2] + twins[1] + twins[-1]:
+        copy.start()
     pl.when(p > 0)(up1.wait_recv)
     pl.when(p < 3)(down1.wait_recv)
     pl.when((p > 0) & (p < 3))(up2.start)
     pl.when((p > 0) & (p < 3))(down2.start)
-    for copy in c1 + d1:
-        copy.wait_recv()
-    for copy in c2 + d2 + twins[1] + twins[-1]:
-        copy.start()
-    for copy in c2 + d2:
-        copy.wait_recv()
+    for o in c2:
+        for copy in c2[o]:
+            copy.wait_recv()
     for copy in twins[2]:
         copy.start()
-    pl.when(p > 1)(up2.wait_recv)
-    pl.when(p < 2)(down2.wait_recv)
-    pl.when(p == 2)(up3.start)
-    pl.when(p == 1)(down3.start)
     for d in (0, 1, -1, 2):
         for copy in twins[d]:
             copy.wait_recv()
@@ -348,6 +350,10 @@
         if q >= 1:
             dispatch(q - 1)
     dispatch(CHUNKS - 1)
+    pl.when(p > 1)(up2.wait_recv)
+    pl.when(p < 2)(down2.wait_recv)
+    pl.when(p == 2)(up3.start)
+    pl.when(p == 1)(down3.start)
 
     pl.when(p == 3)(up3.wait_recv)
     pl.when(p == 0)(down3.wait_recv)
@@ -442,8 +448,11 @@
             copy.wait_send()
         whole(sent, got, q, p_send, p_recv).wait_send()
         whole(made, back, q, r_send, r_recv).wait_send()
-    for copy in kv_steps + z_copies + meta_copies + a1 + b1 + a2 + b2 + c1 + d1 + c2 + d2:
+    for copy in kv_steps + z_copies + meta_copies + a1 + b1 + a2 + b2:
         copy.wait_send()
+    for o in c1:
+        for copy in c1[o] + c2[o]:
+            copy.wait_send()
     for d in (0, 1, -1, 2):
         for copy in twins[d]:
             copy.wait_send()
@@ -478,7 +487,7 @@
             full(2, slots, units), half(slots, units),
             half(CHUNKS, slots, width), half(CHUNKS, slots, width),
             full(CHUNKS, 256, width), half(CHUNKS, 3, 64, width), half(CHUNKS, 3, 64, width),
-            dma(48), dma(48), dma(13),
+            dma(80), dma(80), dma(13),
             dma(CHUNKS, 2), dma(CHUNKS, 2), dma(CHUNKS, 2), dma(CHUNKS, 2),
             dma(CHUNKS), dma(CHUNKS), dma(CHUNKS), dma(CHUNKS),
             dma(CHUNKS, 2), dma(CHUNKS, 2), dma(CHUNKS, 2), dma(CHUNKS, 2),

time: 289 us -> 261 us (0.903)
  the two profiles are of different devices: /device:TPU:48 before, /device:TPU:64 now
where the time goes in v3:
time: 261 us; the launch traced here: 260 us
  Pallas kernels  254 us (97%)
  local copies, waits for them, and re-layouts  6.12 us (2%)
    pallas_call x1, Pallas kernels, layer(): pl.pallas_call(layer_kernel, out_shape=(jax.ShapeDtypeStruct((64, d), jnp...  254 us

profile of v3, /device:TPU:64, one launch (start us, length us, event | category | flops | bytes accessed | tf_op | source)
XLA Modules:
  0.0 260.4 jit_solution(3279861465676907914)
XLA Ops:
  0.6 0.8 pad_dynamic-slice_fusion
  1.4 0.6 broadcast_in_dim.12.span_hbm
  2.0 1.5 copy.15
  3.4 253.7 %shard_map.140 = (bf16[64,2048]{1,0:T(8,128)(2,1)}, bf16[64,2048]{1,0:T(8,128)(2,1)}) custom-call(bf16[64,4096]{1,0:T(8,128)(2,1)} %bitcast.24, bf16[64,512]{1,0:T(8,128)(2,1)} %bitcast.29, bf16[64,512]{1,0:T(8,128)(2,1)} %bitcast.30, s32[1,320]{1,0:T(1,128)} %broadcast_in_dim.12.span_hbm, bf16[64,2048]{1,0:T(8,128)(2,1)} %bitcast.28, f32[1,2048]{1,0:T(1,128)} %bitcast.31, ...), custom_call_target="tpu_custom_call" | custom-call | flops 7000000000 | bytes 30000000 | tf_op jit(solution)/shard_map/pallas_call | solution.py:475
  257.1 1.7 copy.18
  258.8 1.7 copy.19

commit v4 on v3

--- a/solution.py
+++ b/solution.py
@@ -12,6 +12,8 @@
 PLANE = X * Y * CORES
 SUB = 4
 CHUNKS = 4
+BATCH = 2 * CAP
+STEPS = 2 * CHUNKS
 EPSILON = 1e-06
 NEG = -1e30
 ANY = pl.BlockSpec(memory_space=pl.ANY)
@@ -42,7 +44,7 @@
     q_hbm, k_hbm, v_hbm, span_hbm, res_hbm, gain_hbm, logits_hbm, ids_hbm, keep_hbm, wout_ref, wg_ref, wu_ref, wd_ref,
     hidden_ref, out_ref,
     q_ref, kv, span_ref, res_ref, gain_ref, logits_ref, ids_ref, keep_ref, meta, metas,
-    wbuf, att, total, wv, pick, comb, tok, sent, got, accum, act, made, back, part, far, home,
+    wbuf, att, total, wv, pick, comb, tok, sent, got, accum, act, made, back, own, far, home,
     send, recv, local,
     z_send, z_recv, h_send, h_recv, p_send, p_recv, r_send, r_recv, f_send, f_recv, o_send, o_recv,
 ):
@@ -76,8 +78,8 @@
             src_ref=src, dst_ref=dst, send_sem=ss, recv_sem=rs, device_id=peer, device_id_type=MESH
         )
 
-    def block(owner):
-        return wv.at[:, rows(96 * ((owner + SUB) % SUB), 96)]
+    def block(m, owner):
+        return wv.at[m, rows(96 * ((owner + SUB) % SUB), 96)]
 
     ja = (y * 2 + c) * X + x
     jb = (x * 2 + c) * Y + y
@@ -143,24 +145,36 @@
             meta[half, PLANE + group * i:PLANE + group * (i + 1)] = weight[chunk]
     metas[0] = meta[zh]
     meta_copies = [
-        remote(meta.at[1 - zh], metas.at[3], at(dz=8)),
-        remote(meta.at[((z + 4) % Z) // LINE], metas.at[1], at(dz=4)),
-        remote(meta.at[((z + 12) % Z) // LINE], metas.at[2], at(dz=-4)),
+        remote(meta.at[1 - zh], metas.at[1], at(dz=8)),
+        remote(meta.at[((z + 4) % Z) // LINE], metas.at[2], at(dz=4)),
+        remote(meta.at[((z + 12) % Z) // LINE], metas.at[3], at(dz=-4)),
     ]
     for copy in meta_copies:
         copy.start()
 
-    for copy in z_copies:
-        copy.wait_recv()
     kv_steps[0].wait_recv()
     kv_steps[1].start()
-
-    up1 = remote(block(p), block(p), at(dz=1))
-    down1 = remote(block(p), block(p), at(dz=-1))
-    up2 = remote(block(p - 1), block(p - 1), at(dz=1))
-    down2 = remote(block(p + 1), block(p + 1), at(dz=-1))
-    up3 = remote(block(0), block(0), at(dz=1))
-    down3 = remote(block(3), block(3), at(dz=-1))
+    for copy in z_copies:
+        copy.wait_recv()
+
+    up1 = [remote(block(m, p), block(m, p), at(dz=1)) for m in range(3)]
+    down1 = [remote(block(m, p), block(m, p), at(dz=-1)) for m in range(3)]
+    up2 = [remote(block(m, p - 1), block(m, p - 1), at(dz=1)) for m in range(3)]
+    down2 = [remote(block(m, p + 1), block(m, p + 1), at(dz=-1)) for m in range(3)]
+    up3 = [remote(block(m, 0), block(m, 0), at(dz=1)) for m in range(3)]
+    down3 = [remote(block(m, 3), block(m, 3), at(dz=-1)) for m in range(3)]
+
+    def pass_on(m):
+        pl.when(p > 0)(up1[m].wait_recv)
+        pl.when(p < 3)(down1[m].wait_recv)
+        pl.when((p > 0) & (p < 3))(up2[m].start)
+        pl.when((p > 0) & (p < 3))(down2[m].start)
+
+    def pass_last(m):
+        pl.when(p > 1)(up2[m].wait_recv)
+        pl.when(p < 2)(down2[m].wait_recv)
+        pl.when(p == 2)(up3[m].start)
+        pl.when(p == 1)(down3[m].start)
 
     def piece_a(dx, dy, lo, n):
         return wbuf.at[pl.ds(lo, n), rows(16 * ((((y + dy + Y) % Y) * 2 + c) * X + (x + dx + X) % X), 16)]
@@ -196,8 +210,9 @@
         copy.start()
     for load in loads[7:10]:
         load.wait()
-    pl.when(p < 3)(up1.start)
-    pl.when(p > 0)(down1.start)
+    for m in range(3):
+        pl.when(p < 3)(up1[m].start)
+        pl.when(p > 0)(down1[m].start)
     for copy in a1 + b1:
         copy.wait_recv()
     for copy in a2 + b2 + c1[1] + c1[-1]:
@@ -221,16 +236,11 @@
         lane = lax.broadcasted_iota(jnp.int32, (PLANE, 128), 1)
         slots = jnp.where(lane < 64, metas[2 * a, 0:PLANE], metas[2 * a + 1, 0:PLANE])
         weights = jnp.where(lane < 64, metas[2 * a, PLANE:], metas[2 * a + 1, PLANE:])
-        row = lax.broadcasted_iota(jnp.int32, (PLANE, 4 * CAP, 128), 1)
-        column = lax.broadcasted_iota(jnp.int32, (PLANE, 4 * CAP, 128), 2)
-        same = row // CAP == 2 * a + column // 64
-        hit = same & (slots[:, None, :] == (row % CAP).astype(jnp.float32))
-        pick[:, 128 * a:128 * (a + 1)] = (
-            jnp.where(hit, 1.0, 0.0).reshape(PLANE * 4 * CAP, 128).astype(jnp.bfloat16)
-        )
-        comb[:, 128 * a:128 * (a + 1)] = (
-            jnp.where(hit, weights[:, None, :], 0.0).reshape(PLANE * 4 * CAP, 128).astype(jnp.bfloat16)
-        )
+        row = lax.broadcasted_iota(jnp.int32, (PLANE, BATCH, 128), 1)
+        column = lax.broadcasted_iota(jnp.int32, (PLANE, BATCH, 128), 2)
+        hit = (row // CAP == column // 64) & (slots[:, None, :] == (row % CAP).astype(jnp.float32))
+        pick[a] = jnp.where(hit, 1.0, 0.0).reshape(PLANE * BATCH, 128).astype(jnp.bfloat16)
+        comb[a] = jnp.where(hit, weights[:, None, :], 0.0).reshape(PLANE * BATCH, 128).astype(jnp.bfloat16)
 
     docs = lax.broadcasted_iota(jnp.int32, (8, 320), 0)
     key_doc = jnp.where(docs == span_ref[...], 1.0, 0.0).astype(jnp.bfloat16)
@@ -241,8 +251,8 @@
     query_at = lax.broadcasted_iota(jnp.int32, (64, 320), 0)
     bias = jnp.where((key_at <= query_at + 256) & (same_doc > 0.5), 0.0, NEG)
     loads[10].wait()
-    kv_steps[3].wait_recv()
-    for g in range(4):
+
+    def attend(g):
         head = lambda h: (g * 8 + h) * HD
         queries = jnp.concatenate([q_ref[:, head(h):head(h) + HD] for h in range(8)], axis=0)
         keys = kv[:, 0, :, g * HD:(g + 1) * HD].reshape(5 * 64, HD)
@@ -261,19 +271,21 @@
         copy.wait_recv()
     for copy in c2[1] + c2[-1]:
         copy.start()
+    pass_on(0)
     for copy in c1[2]:
         copy.wait_recv()
     for copy in c2[2] + twins[1] + twins[-1]:
         copy.start()
-    pl.when(p > 0)(up1.wait_recv)
-    pl.when(p < 3)(down1.wait_recv)
-    pl.when((p > 0) & (p < 3))(up2.start)
-    pl.when((p > 0) & (p < 3))(down2.start)
+    pass_on(1)
+    kv_steps[3].wait_recv()
+    for g in range(4):
+        attend(g)
     for o in c2:
         for copy in c2[o]:
             copy.wait_recv()
     for copy in twins[2]:
         copy.start()
+    pass_on(2)
     for d in (0, 1, -1, 2):
         for copy in twins[d]:
             copy.wait_recv()
@@ -296,106 +308,120 @@
 
     near = [
         (
-            copy_to(tok.at[q, pl.ds(0, 64)], tok.at[q, pl.ds(64, 64)], z_send.at[q, 0], z_recv.at[q, 0], at(dz=4)),
-            copy_to(tok.at[q, pl.ds(0, 64)], tok.at[q, pl.ds(128, 64)], z_send.at[q, 1], z_recv.at[q, 1], at(dz=-4)),
+            copy_to(tok.at[q, pl.ds(0, 64)], tok.at[q, pl.ds(128, 64)], z_send.at[q, 0], z_recv.at[q, 0], at(dz=4)),
+            copy_to(tok.at[q, pl.ds(0, 64)], tok.at[q, pl.ds(192, 64)], z_send.at[q, 1], z_recv.at[q, 1], at(dz=-4)),
         )
         for q in range(CHUNKS)
     ]
     across = [
         (
-            copy_to(tok.at[q, pl.ds(64, 32)], tok.at[q, pl.ds(192, 32)], h_send.at[q, 0], h_recv.at[q, 0], at(dz=4)),
-            copy_to(tok.at[q, pl.ds(160, 32)], tok.at[q, pl.ds(224, 32)], h_send.at[q, 1], h_recv.at[q, 1], at(dz=-4)),
+            copy_to(tok.at[q, pl.ds(128, 32)], tok.at[q, pl.ds(64, 32)], h_send.at[q, 0], h_recv.at[q, 0], at(dz=4)),
+            copy_to(tok.at[q, pl.ds(224, 32)], tok.at[q, pl.ds(96, 32)], h_send.at[q, 1], h_recv.at[q, 1], at(dz=-4)),
         )
         for q in range(CHUNKS)
     ]
-    for q in range(CHUNKS):
-        for copy in near[q]:
-            copy.start()
+    for copy in near[0]:
+        copy.start()
     hidden_ref[...] = hidden.astype(jnp.bfloat16)
 
-    def spread(src, dst, q, ss, rs):
+    def spread(src, dst, i, ss, rs):
         def go(o, _):
             peer, where = partner(o)
             copy_to(
-                src.at[q, rows(32 * peer, 32)], dst.at[q, rows(32 * me, 32)], ss.at[q], rs.at[q], where
+                src.at[i, rows(BATCH * peer, BATCH)], dst.at[i, rows(BATCH * me, BATCH)], ss.at[i], rs.at[i], where
             ).start()
             return 0
 
         lax.fori_loop(1, PLANE, go, 0)
-        dst[q, rows(32 * me, 32)] = src[q, rows(32 * me, 32)]
-
-    def whole(src, dst, q, ss, rs):
-        every = pl.ds(0, 32 * (PLANE - 1))
-        return copy_to(src.at[q, every], dst.at[q, every], ss.at[q], rs.at[q], at(dz=1))
-
-    def dispatch(q):
-        for copy in across[q]:
-            copy.wait_recv()
-
+        dst[i, rows(BATCH * me, BATCH)] = src[i, rows(BATCH * me, BATCH)]
+
+    def whole(src, dst, i, ss, rs):
+        every = pl.ds(0, BATCH * (PLANE - 1))
+        return copy_to(src.at[i, every], dst.at[i, every], ss.at[i], rs.at[i], at(dz=1))
+
+    def tile_rows(i):
+        return pl.ds(pl.multiple_of(i * 256, 256), 256)
+
+    def dispatch(b, q):
         def tile(i, _):
-            part_rows = pl.ds(pl.multiple_of(i * 256, 256), 256)
-            sent[q, part_rows] = jnp.dot(
-                pick[part_rows], tok[q], preferred_element_type=jnp.float32
+            sent[b * CHUNKS + q, tile_rows(i)] = jnp.dot(
+                pick[b, tile_rows(i)], tok[q, 128 * b:128 * (b + 1)], preferred_element_type=jnp.float32
             ).astype(jnp.bfloat16)
             return 0
 
-        lax.fori_loop(0, 4, tile, 0)
-        spread(sent, got, q, p_send, p_recv)
+        lax.fori_loop(0, 2, tile, 0)
+        spread(sent, got, b * CHUNKS + q, p_send, p_recv)
 
     for q in range(CHUNKS):
+        if q < CHUNKS - 1:
+            for copy in near[q]:
+                copy.wait_send()
+            for copy in near[q + 1]:
+                copy.start()
         for copy in near[q]:
             copy.wait_recv()
         for copy in across[q]:
             copy.start()
+        dispatch(1, q)
         if q >= 1:
-            dispatch(q - 1)
-    dispatch(CHUNKS - 1)
-    pl.when(p > 1)(up2.wait_recv)
-    pl.when(p < 2)(down2.wait_recv)
-    pl.when(p == 2)(up3.start)
-    pl.when(p == 1)(down3.start)
-
-    pl.when(p == 3)(up3.wait_recv)
-    pl.when(p == 0)(down3.wait_recv)
+            for copy in across[q - 1]:
+                copy.wait_recv()
+            dispatch(0, q - 1)
+    for copy in across[CHUNKS - 1]:
+        copy.wait_recv()
+    dispatch(0, CHUNKS - 1)
+    for m in range(3):
+        pass_last(m)
+
+    def last_here(m):
+        pl.when(p == 3)(up3[m].wait_recv)
+        pl.when(p == 0)(down3[m].wait_recv)
+
+    last_here(0)
+    last_here(1)
     transposed = (((1,), (1,)), ((), ()))
-    for q in range(CHUNKS):
-        whole(sent, got, q, p_send, p_recv).wait_recv()
+
+    def gate_up(b, q):
+        step = b * CHUNKS + q
+        whole(sent, got, step, p_send, p_recv).wait_recv()
         cols = slice(width * q, width * (q + 1))
 
-        def tile(i, _, q=q, cols=cols):
-            part_rows = pl.ds(pl.multiple_of(i * 256, 256), 256)
+        def tile(i, _):
             for m in range(2):
                 value = lax.dot_general(
-                    got[q, part_rows], wv[m, :, cols], transposed, preferred_element_type=jnp.float32
+                    got[step, tile_rows(i)], wv[m, :, cols], transposed, preferred_element_type=jnp.float32
                 )
                 if q == 0:
-                    accum[m, part_rows] = value
+                    accum[b, m, tile_rows(i)] = value
                 else:
-                    accum[m, part_rows] += value
+                    accum[b, m, tile_rows(i)] += value
             return 0
 
-        lax.fori_loop(0, 4, tile, 0)
-
-    def activate(i, _):
-        part_rows = pl.ds(pl.multiple_of(i * 256, 256), 256)
-        gate = accum[0, part_rows]
-        act[part_rows] = (gate / (1.0 + jnp.exp(-gate)) * accum[1, part_rows]).astype(jnp.bfloat16)
-        return 0
-
-    lax.fori_loop(0, 4, activate, 0)
-
-    for q in range(CHUNKS):
+        lax.fori_loop(0, 2, tile, 0)
+
+    def activate(b):
+        def tile(i, _):
+            gate = accum[b, 0, tile_rows(i)]
+            act[b, tile_rows(i)] = (gate / (1.0 + jnp.exp(-gate)) * accum[b, 1, tile_rows(i)]).astype(jnp.bfloat16)
+            return 0
+
+        lax.fori_loop(0, 2, tile, 0)
+
+    def down(b, q):
         cols = slice(width * q, width * (q + 1))
 
-        def tile(i, _, q=q, cols=cols):
-            part_rows = pl.ds(pl.multiple_of(i * 256, 256), 256)
-            made[q, part_rows] = jnp.dot(
-                act[part_rows], wv[2, :, cols], preferred_element_type=jnp.float32
+        def tile(i, _):
+            made[b * CHUNKS + q, tile_rows(i)] = jnp.dot(
+                act[b, tile_rows(i)], wv[2, :, cols], preferred_element_type=jnp.float32
             ).astype(jnp.bfloat16)
             return 0
 
-        lax.fori_loop(0, 4, tile, 0)
-        spread(made, back, q, r_send, r_recv)
+        lax.fori_loop(0, 2, tile, 0)
+
+    def give_back(step):
+        if step > 0:
+            whole(made, back, step - 1, r_send, r_recv).wait_send()
+        spread(made, back, step, r_send, r_recv)
 
     def half_copies(q):
         return (
@@ -409,65 +435,93 @@
             copy_to(far.at[q, 2], home.at[q, 2], o_send.at[q, 1], o_recv.at[q, 1], at(dz=4)),
         )
 
-    def combine(q):
-        whole(made, back, q, r_send, r_recv).wait_recv()
-        part[q] = lax.dot_general(
-            comb[...], back[q], (((0,), (0,)), ((), ())), preferred_element_type=jnp.float32
+    def combine(b, q):
+        step = b * CHUNKS + q
+        whole(made, back, step, r_send, r_recv).wait_recv()
+        part = lax.dot_general(
+            comb[b], back[step], (((0,), (0,)), ((), ())), preferred_element_type=jnp.float32
         )
-        far[q, 0] = part[q, 192:256].astype(jnp.bfloat16)
-        for copy in half_copies(q):
-            copy.start()
-
-    def relay(q):
-        for copy in half_copies(q):
-            copy.wait_recv()
-        ahead, behind = part[q, 128:192], part[q, 64:128]
-        far[q, 2, 0:32] = (ahead[0:32] + home[q, 0, 0:32].astype(jnp.float32)).astype(jnp.bfloat16)
-        far[q, 2, 32:64] = ahead[32:64].astype(jnp.bfloat16)
-        far[q, 1, 0:32] = behind[0:32].astype(jnp.bfloat16)
-        far[q, 1, 32:64] = (behind[32:64] + home[q, 0, 32:64].astype(jnp.float32)).astype(jnp.bfloat16)
-        for copy in home_copies(q):
-            copy.start()
+        if b == 0:
+            own[q] = part[0:64]
+            far[q, 0] = part[64:128].astype(jnp.bfloat16)
+            for copy in half_copies(q):
+                copy.start()
+        else:
+            for copy in half_copies(q):
+                copy.wait_recv()
+            far[q, 1, 0:32] = part[0:32].astype(jnp.bfloat16)
+            far[q, 1, 32:64] = (part[32:64] + home[q, 0, 32:64].astype(jnp.float32)).astype(jnp.bfloat16)
+            far[q, 2, 0:32] = (part[64:96] + home[q, 0, 0:32].astype(jnp.float32)).astype(jnp.bfloat16)
+            far[q, 2, 32:64] = part[96:128].astype(jnp.bfloat16)
+            for copy in home_copies(q):
+                copy.start()
 
     def finish(q):
         for copy in home_copies(q):
             copy.wait_recv()
-        total = part[q, 0:64] + home[q, 1].astype(jnp.float32) + home[q, 2].astype(jnp.float32)
+        total = own[q] + home[q, 1].astype(jnp.float32) + home[q, 2].astype(jnp.float32)
         out_ref[:, width * q:width * (q + 1)] = total.astype(jnp.bfloat16)
 
-    for step in range(CHUNKS + 2):
-        if step < CHUNKS:
-            combine(step)
-        if 0 <= step - 1 < CHUNKS:
-            relay(step - 1)
-        if 0 <= step - 2 < CHUNKS:
-            finish(step - 2)
-
     for q in range(CHUNKS):
-        for copy in near[q] + across[q] + half_copies(q) + home_copies(q):
+        gate_up(1, q)
+        gate_up(0, q)
+    activate(0)
+    last_here(2)
+    down(0, 0)
+    give_back(0)
+    for q in range(1, CHUNKS):
+        down(0, q)
+    give_back(1)
+    activate(1)
+    give_back(2)
+    combine(0, 0)
+    down(1, 0)
+    down(1, 1)
+    give_back(3)
+    combine(0, 1)
+    down(1, 2)
+    down(1, 3)
+    give_back(4)
+    combine(0, 2)
+    give_back(5)
+    combine(0, 3)
+    give_back(6)
+    combine(1, 0)
+    give_back(7)
+    combine(1, 1)
+    finish(0)
+    combine(1, 2)
+    finish(1)
+    combine(1, 3)
+    finish(2)
+    finish(3)
+
+    for copy in near[CHUNKS - 1]:
+        copy.wait_send()
+    for q in range(CHUNKS):
+        for copy in across[q] + half_copies(q) + home_copies(q):
             copy.wait_send()
-        whole(sent, got, q, p_send, p_recv).wait_send()
-        whole(made, back, q, r_send, r_recv).wait_send()
+    for step in range(STEPS):
+        whole(sent, got, step, p_send, p_recv).wait_send()
+    whole(made, back, STEPS - 1, r_send, r_recv).wait_send()
     for copy in kv_steps + z_copies + meta_copies + a1 + b1 + a2 + b2:
         copy.wait_send()
     for o in c1:
-        for copy in c1[o] + c2[o]:
+        for copy in c1[o] + c2[o] + twins[o]:
             copy.wait_send()
-    for d in (0, 1, -1, 2):
-        for copy in twins[d]:
-            copy.wait_send()
-    pl.when(p < 3)(up1.wait_send)
-    pl.when(p > 0)(down1.wait_send)
-    pl.when((p > 0) & (p < 3))(up2.wait_send)
-    pl.when((p > 0) & (p < 3))(down2.wait_send)
-    pl.when(p == 2)(up3.wait_send)
-    pl.when(p == 1)(down3.wait_send)
+    for m in range(3):
+        pl.when(p < 3)(up1[m].wait_send)
+        pl.when(p > 0)(down1[m].wait_send)
+        pl.when((p > 0) & (p < 3))(up2[m].wait_send)
+        pl.when((p > 0) & (p < 3))(down2[m].wait_send)
+        pl.when(p == 2)(up3[m].wait_send)
+        pl.when(p == 1)(down3[m].wait_send)
 
 
 def layer(*args):
     d = args[4].shape[1]
     width = d // CHUNKS
-    slots = PLANE * 4 * CAP
+    slots = PLANE * BATCH
     units = SUB * 96
     dma = lambda *shape: pltpu.SemaphoreType.DMA(shape)
     half = lambda *shape: pltpu.VMEM(shape, jnp.bfloat16)
@@ -482,14 +536,14 @@
             full(64, 64), pltpu.VMEM((8, 64), jnp.int32), pltpu.VMEM((8, 64), jnp.int32),
             full(2, 64, 128), full(4, 64, 128),
             half(LINE, 512, d), half(64, 4096), full(64, d), half(3, units, d),
-            half(slots, 256), half(slots, 256), half(CHUNKS, 256, width),
-            half(CHUNKS, slots, width), half(CHUNKS, slots, width),
-            full(2, slots, units), half(slots, units),
-            half(CHUNKS, slots, width), half(CHUNKS, slots, width),
-            full(CHUNKS, 256, width), half(CHUNKS, 3, 64, width), half(CHUNKS, 3, 64, width),
-            dma(80), dma(80), dma(13),
+            half(2, slots, 128), half(2, slots, 128), half(CHUNKS, 256, width),
+            half(STEPS, slots, width), half(STEPS, slots, width),
+            full(2, 2, slots, units), half(2, slots, units),
+            half(STEPS, slots, width), half(STEPS, slots, width),
+            full(CHUNKS, 64, width), half(CHUNKS, 3, 64, width), half(CHUNKS, 3, 64, width),
+            dma(96), dma(96), dma(13),
             dma(CHUNKS, 2), dma(CHUNKS, 2), dma(CHUNKS, 2), dma(CHUNKS, 2),
-            dma(CHUNKS), dma(CHUNKS), dma(CHUNKS), dma(CHUNKS),
+            dma(STEPS), dma(STEPS), dma(STEPS), dma(STEPS),
             dma(CHUNKS, 2), dma(CHUNKS, 2), dma(CHUNKS, 2), dma(CHUNKS, 2),
         ],
         compiler_params=pltpu.CompilerParams(

time: 261 us -> 244 us (0.935)
  the two profiles are of different devices: /device:TPU:64 before, /device:TPU:50 now
where the time goes in v4:
time: 244 us
  Pallas kernels  237 us (97%)
  local copies, waits for them, and re-layouts  6.12 us (3%)
    pallas_call x1, Pallas kernels, layer(): pl.pallas_call(layer_kernel, out_shape=(jax.ShapeDtypeStruct((64, d), jnp...  237 us

profile of v4, /device:TPU:50, one launch (start us, length us, event | category | flops | bytes accessed | tf_op | source)
XLA Modules:
  0.0 243.5 jit_solution(2235942070338616386)
XLA Ops:
  0.6 0.8 pad_dynamic-slice_fusion
  1.4 0.6 broadcast_in_dim.12.span_hbm
  2.0 1.5 copy.15
  3.4 236.7 %shard_map.140 = (bf16[64,2048]{1,0:T(8,128)(2,1)}, bf16[64,2048]{1,0:T(8,128)(2,1)}) custom-call(bf16[64,4096]{1,0:T(8,128)(2,1)} %bitcast.24, bf16[64,512]{1,0:T(8,128)(2,1)} %bitcast.29, bf16[64,512]{1,0:T(8,128)(2,1)} %bitcast.30, s32[1,320]{1,0:T(1,128)} %broadcast_in_dim.12.span_hbm, bf16[64,2048]{1,0:T(8,128)(2,1)} %bitcast.28, f32[1,2048]{1,0:T(1,128)} %bitcast.31, ...), custom_call_target="tpu_custom_call" | custom-call | flops 7000000000 | bytes 30000000 | tf_op jit(solution)/shard_map/pallas_call | solution.py:529
  240.2 1.7 copy.18
  241.8 1.7 copy.19

commit v5 on v4

--- a/solution.py
+++ b/solution.py
@@ -18,7 +18,6 @@
 NEG = -1e30
 ANY = pl.BlockSpec(memory_space=pl.ANY)
 VMEM = pl.BlockSpec(memory_space=pltpu.VMEM)
-Z_OFFSETS = (1, -1, 2, -2, 3, -3, 4)
 
 
 def place():
@@ -83,8 +82,13 @@
 
     ja = (y * 2 + c) * X + x
     jb = (x * 2 + c) * Y + y
+
+    def slice_piece(d):
+        t = (s - d + LINE) % LINE
+        return wbuf.at[t, rows(jnp.where(t < 4, ja, jb) * 16, 16)]
+
     mine = jnp.where(s < 4, ja, jb) * 16
-    piece = wbuf.at[s, rows(mine, 16)]
+    piece = slice_piece(0)
     moves = [
         (k_hbm, kv.at[4, 0]), (v_hbm, kv.at[4, 1]), (wout_ref.at[rows(mine, 16)], piece),
         (ids_hbm, ids_ref), (keep_hbm, keep_ref), (logits_hbm, logits_ref), (span_hbm, span_ref),
@@ -108,15 +112,21 @@
     pl.semaphore_wait(barrier, 9 + PLANE - 1)
 
     kv_steps = [remote(kv.at[4 - d], kv.at[3 - d], at(dz=1)) for d in range(4)]
-    z_copies = [remote(piece, piece, at(dz=d)) for d in Z_OFFSETS]
+    z_up = [remote(slice_piece(d), slice_piece(d), at(dz=1)) for d in range(4)]
+    z_down = [remote(slice_piece(-d), slice_piece(-d), at(dz=-1)) for d in range(3)]
+    z_copies = z_up + z_down
     for load in loads[:3]:
         load.wait()
-    for copy in z_copies:
-        copy.start()
+    z_up[0].start()
+    z_down[0].start()
     kv_steps[0].start()
 
     for load in loads[3:7]:
         load.wait()
+    z_up[0].wait_recv()
+    z_up[1].start()
+    z_down[0].wait_recv()
+    z_down[1].start()
     experts = logits_ref.shape[1]
     expert = lax.broadcasted_iota(jnp.int32, (experts, 64), 0)
     named = expert == ids_ref[0:1, :]
@@ -132,9 +142,23 @@
         preferred_element_type=jnp.float32,
     )
     slot = jnp.where(kept, before, -1.0)
-    chosen = jnp.where(named, logits_ref[...], -jnp.inf)
+    same = lax.broadcasted_iota(jnp.int32, (64, 64), 0) == lax.broadcasted_iota(jnp.int32, (64, 64), 1)
+    identity = jnp.where(same, 1.0, 0.0).astype(jnp.bfloat16)
+    rest = logits_ref[...]
+    logits = jnp.zeros((experts, 64), jnp.float32)
+    for _ in range(3):
+        high = rest.astype(jnp.bfloat16)
+        rest = rest - high.astype(jnp.float32)
+        logits = logits + lax.dot_general(
+            high, identity, (((0,), (0,)), ((), ())), preferred_element_type=jnp.float32
+        )
+    chosen = jnp.where(named, logits, -jnp.inf)
     terms = jnp.exp(chosen - jnp.max(chosen, axis=0, keepdims=True))
     weight = jnp.where(kept, terms / jnp.sum(terms, axis=0, keepdims=True), 0.0)
+    z_up[1].wait_recv()
+    z_up[2].start()
+    z_down[1].wait_recv()
+    z_down[2].start()
     slot = jnp.concatenate([slot, slot], axis=1)
     weight = jnp.concatenate([weight, weight], axis=1)
     group = Y * CORES
@@ -152,10 +176,12 @@
     for copy in meta_copies:
         copy.start()
 
+    z_up[2].wait_recv()
+    z_up[3].start()
+    z_down[2].wait_recv()
     kv_steps[0].wait_recv()
     kv_steps[1].start()
-    for copy in z_copies:
-        copy.wait_recv()
+    z_up[3].wait_recv()
 
     up1 = [remote(block(m, p), block(m, p), at(dz=1)) for m in range(3)]
     down1 = [remote(block(m, p), block(m, p), at(dz=-1)) for m in range(3)]
@@ -561,7 +587,7 @@
     doc = jnp.pad(doc_ids[0], (256, 0), constant_values=-1)
     span = lax.dynamic_slice(doc, (64 * s,), (320,))[None]
     hidden, out = layer(
-        queries[0], key_heads[0], value_heads[0], span, residual[0], norm_gain[None], router_logits[0].T,
+        queries[0], key_heads[0], value_heads[0], span, residual[0], norm_gain[None], router_logits[0],
         expert_ids[0].T, keep_mask[0].T, w_out, w_gate[0], w_up[0], w_down[0],
     )
     return hidden[None], out[None]

time: 244 us -> 234 us (0.959)
  the two profiles are of different devices: /device:TPU:50 before, /device:TPU:64 now
where the time goes in v5:
time: 234 us
  Pallas kernels  229 us (98%)
  local copies, waits for them, and re-layouts  4.67 us (2%)
    pallas_call x1, Pallas kernels, layer(): pl.pallas_call(layer_kernel, out_shape=(jax.ShapeDtypeStruct((64, d), jnp...  229 us

profile of v5, /device:TPU:64, one launch (start us, length us, event | category | flops | bytes accessed | tf_op | source)
XLA Modules:
  0.0 234.1 jit_solution(17585049680569574943)
XLA Ops:
  0.6 0.8 pad_dynamic-slice_fusion
  1.4 0.6 broadcast_in_dim.12.span_hbm
  2.0 228.8 %shard_map.140 = (bf16[64,2048]{1,0:T(8,128)(2,1)}, bf16[64,2048]{1,0:T(8,128)(2,1)}) custom-call(bf16[64,4096]{1,0:T(8,128)(2,1)} %bitcast.21, bf16[64,512]{1,0:T(8,128)(2,1)} %bitcast.26, bf16[64,512]{1,0:T(8,128)(2,1)} %bitcast.27, s32[1,320]{1,0:T(1,128)} %broadcast_in_dim.12.span_hbm, bf16[64,2048]{1,0:T(8,128)(2,1)} %bitcast.25, f32[1,2048]{1,0:T(1,128)} %bitcast.29, ...), custom_call_target="tpu_custom_call" | custom-call | flops 7000000000 | bytes 30000000 | tf_op jit(solution)/shard_map/pallas_call | solution.py:555
  230.7 1.7 copy.17
  232.4 1.7 copy.18
